TPU v7x, 32 devices: a whole 2x2x4 slice. The times are simulated.
32 devices in a mesh: row: 4 (over x, core), col: 8 (over z, y).
Axes of the slice: x: 2, y: 2, z: 4, core: 2. Of those that a mesh axis runs over, the one named last changes fastest.
Arguments:
- amplitudes: bfloat16 [2048, 16384], P(('row', 'col')), may hold values from -6 to 6
- integrals: bfloat16 [8192, 16384], P('col', 'row'), may hold values from -0.21875 to 0.21875
- orbital_irrep: int32 [1024], replicated, may hold values from 0 to 7
- orbital_spin: int32 [1024], replicated, may hold values from 0 to 1
Outputs:
- residual_tiles: bfloat16 [2048, 8192], P('row', 'col')
All inputs are finite; a program needn't handle non-finite values.
Results may differ from a plain program's by a relative error of at most 0.001.
Values may be sent and summed in bfloat16 or wider, within the bound.
No kernel may reach another device: no remote copies, remote signals or barrier semaphores. Data moves between devices by JAX's collectives and lax.ppermute only.
A program may use at most 128 MiB of HBM per device.

v0:
```python
import jax
import jax.numpy as jnp
from jax import lax
from jax.sharding import PartitionSpec as P


def pair_labels(first, count, orbital_irrep, orbital_spin):
    lead_irrep = lax.dynamic_slice_in_dim(orbital_irrep, first, count, 0)
    lead_spin = lax.dynamic_slice_in_dim(orbital_spin, first, count, 0)
    labels = jnp.bitwise_xor(lead_irrep[:, None], orbital_irrep[None, :]) + 8 * (
        lead_spin[:, None] + orbital_spin[None, :]
    )
    return labels.reshape(-1)


def local(amplitudes, integrals, orbital_irrep, orbital_spin):
    virtuals = orbital_irrep.shape[0]
    a_count = integrals.shape[0] // virtuals
    c_count = integrals.shape[1] // virtuals
    ab_labels = pair_labels(lax.axis_index("col") * a_count, a_count, orbital_irrep, orbital_spin)
    cd_labels = pair_labels(lax.axis_index("row") * c_count, c_count, orbital_irrep, orbital_spin)
    masked = jnp.where(
        ab_labels[:, None] == cd_labels[None, :], integrals, jnp.zeros((), integrals.dtype)
    )
    grid_rows = lax.all_gather(amplitudes, "col", axis=0, tiled=True)
    regrouped = lax.all_to_all(grid_rows, "row", split_axis=1, concat_axis=0, tiled=True)
    partial_sums = lax.dot_general(
        regrouped, masked, (((1,), (1,)), ((), ())), preferred_element_type=jnp.float32
    )
    return lax.psum_scatter(partial_sums, "row", scatter_dimension=0, tiled=True).astype(
        jnp.bfloat16
    )


def solution(mesh):
    placed = (P(("row", "col"), None), P("col", "row"), P(), P())
    return jax.shard_map(
        local, mesh=mesh, in_specs=placed, out_specs=P("row", "col"), check_vma=False
    )
```

profile of v0, /device:TPU:0, one launch (start us, length us, event | category | flops | bytes accessed | tf_op | source)
XLA Modules:
  0.0 576.4 jit_solution(10336820530677310202)
XLA Ops:
  6.5 0.0 all-gather.2.cloned.1.call-start
  6.5 0.7 all-gather.2.cloned.1.call-update
  7.3 232.6 %all-gather.2.cloned.1.call-done = bf16[512,16384]{1,0:T(8,128)(2,1)} async-done(((bf16[64,16384]{1,0:T(8,128)(2,1)}), bf16[512,16384]{1,0:T(8,128)(2,1)}) %all-gather.2.cloned.1.call-update) | async-done | bytes 16777232 | tf_op jit(solution)/shard_map/all_gather | solution.py:25
  239.8 22.4 %copy.10 = bf16[512,16384]{0,1:T(8,128)(2,1)} copy(bf16[512,16384]{1,0:T(8,128)(2,1)} %all-gather.2.cloned.1.call-done) | data formatting | bytes 33554432 | tf_op jit(solution)/shard_map/all_gather | solution.py:25
  262.2 0.0 copy-start
  262.2 0.0 copy-start.1
  262.2 7.1 %all-to-all-start = ((bf16[512,4,4096]{0,2,1:T(8,128)(2,1)}), bf16[512,4,4096]{0,2,1:T(8,128)(2,1)}, u32[]{:S(2)}, u32[]{:S(2)}) async-start(bf16[512,4,4096]{0,2,1:T(8,128)(2,1)} %bitcast.13), calls=%async_computation | async-start | bytes 33554432 | tf_op jit(solution)/shard_map/all_to_all | solution.py:26
  269.3 0.0 reduce-scatter.2.cloned.1.call-start
  269.4 0.0 copy-done
  269.4 0.1 dynamic_slice.15
  269.5 0.0 copy-done.1
  269.5 0.1 dynamic_slice.14
  269.5 0.6 dynamic_slice.13
  270.1 0.6 dynamic_slice.12
  270.7 0.1 add_bitcast_fusion
  270.8 1.2 multiply_add_fusion
  272.0 180.4 %all-to-all-done = bf16[512,4,4096]{0,2,1:T(8,128)(2,1)} async-done(((bf16[512,4,4096]{0,2,1:T(8,128)(2,1)}), bf16[512,4,4096]{0,2,1:T(8,128)(2,1)}, u32[]{:S(2)}, u32[]{:S(2)}) %all-to-all-start) | async-done | bytes 16777248 | tf_op jit(solution)/shard_map/all_to_all | solution.py:26
  452.4 20.7 %copy.11 = bf16[4,512,4096]{2,1,0:T(8,128)(2,1)} copy(bf16[4,512,4096]{1,2,0:T(8,128)(2,1)} %bitcast.3) | data formatting | bytes 33554432 | tf_op jit(solution)/shard_map/all_to_all | solution.py:26
  473.1 24.2 %fusion.3 = f32[2048,1024]{0,1:T(8,128)} fusion(bf16[2048,4096]{1,0:T(8,128)(2,1)} %bitcast.14, bf16[1024,4096]{1,0:T(8,128)(2,1)} %param.5, s32[4096]{0:T(1024)S(1)} %bitcast.15, s32[1024]{0:T(1024)S(1)} %multiply_add_fusion), kind=kOutput, calls=%fused_computation.4 | convolution fusion | flops 17188257792 | bytes 33574912 | tf_op jit(solution)/shard_map/dot_general | solution.py:27
  497.3 0.0 reduce-scatter.2.cloned.1.call-update
  497.3 69.2 %reduce-scatter.2.cloned.1.call-done = f32[512,1024]{0,1:T(8,128)} async-done(((f32[2048,1024]{0,1:T(8,128)}), f32[512,1024]{0,1:T(8,128)}) %reduce-scatter.2.cloned.1.call-update) | async-done | bytes 2097168 | tf_op jit(solution)/shard_map/reduce_scatter | solution.py:30
  566.5 1.7 convert_element_type.3
  568.2 1.3 copy.12
  (1 shorter events, 0.0 us)
Async XLA Ops:
  6.5 233.3 %all-gather.2.cloned.1.call-start = ((), (), s32[]{:S(2)}) async-start(), calls=%async_computation.2 | async-start | bytes 18874368 | tf_op jit(solution)/shard_map/all_gather | solution.py:25
  262.2 7.2 %copy-start = (s32[1024]{0:T(1024)S(1)}, s32[1024]{0:T(1024)}, u32[]{:S(2)}) copy-start(s32[1024]{0:T(1024)} %param.7) | copy-start | bytes 12292
  262.2 7.3 %copy-start.1 = (s32[1024]{0:T(1024)S(1)}, s32[1024]{0:T(1024)}, u32[]{:S(2)}) copy-start(s32[1024]{0:T(1024)} %param.6) | copy-start | bytes 12292
  262.2 190.2 %all-to-all-start = ((bf16[512,4,4096]{0,2,1:T(8,128)(2,1)}), bf16[512,4,4096]{0,2,1:T(8,128)(2,1)}, u32[]{:S(2)}, u32[]{:S(2)}) async-start(bf16[512,4,4096]{0,2,1:T(8,128)(2,1)} %bitcast.13), calls=%async_computation | async-start | bytes 33554432 | tf_op jit(solution)/shard_map/all_to_all | solution.py:26
  269.3 297.2 %reduce-scatter.2.cloned.1.call-start = ((), (), s32[]{:S(2)}) async-start(), calls=%async_computation.3 | async-start | bytes 10485760 | tf_op jit(solution)/shard_map/reduce_scatter | solution.py:30
Sparse Core Ops, SparseCore 0:
  9.5 230.2 all-gather.1
  497.4 68.9 reduce-scatter.1
where the time goes:
time: 578 us; the launch traced here: 576 us
  waiting for transfers between devices  483 us (84%)
  local copies, waits for them, and re-layouts  45.7 us (8%)
  matrix products  24.2 us (4%)
  between operations  13.4 us (2%)
  starting transfers between devices  7.15 us (1%)
    all_gather x1, waiting for transfers between devices, local(): grid_rows = lax.all_gather(amplitudes, 'col', axis=0, tiled=True)  233 us
    all_to_all x1, waiting for transfers between devices, local(): lax.all_to_all(grid_rows, 'row', split_axis=1, concat_axis=0, tiled=True)  180 us
    reduce_scatter x1, waiting for transfers between devices, local(): lax.psum_scatter(partial_sums, 'row', scatter_dimension=0, tiled=True)  69.2 us
    dot_general x1, matrix products, local(): lax.dot_general(regrouped, masked, (((1,), (1,)), ((), ())), preferred_el...  24.2 us
    all_gather x1, local copies, waits for them, and re-layouts, local(): grid_rows = lax.all_gather(amplitudes, 'col', axis=0, tiled=True)  22.4 us
    all_to_all x1, local copies, waits for them, and re-layouts, local(): lax.all_to_all(grid_rows, 'row', split_axis=1, concat_axis=0, tiled=True)  20.7 us
  transfers between devices with their start and end apart: 3, of which 3 were waited for; matrix products, arithmetic and copies ran while one was open for 0% of the time, Pallas kernels for 0%

commit v1 on v0

v1 whole, which is shorter than its diff:
```python
import functools

import jax
import jax.numpy as jnp
from jax import lax
from jax.experimental import pallas as pl
from jax.experimental.pallas import tpu as pltpu
from jax.sharding import Mesh, PartitionSpec as P

IRREPS = 8
LANES = 128
NT = (((1,), (1,)), ((), ()))


def pair_labels(lead_irrep, lead_spin, irrep, spin):
    return jnp.bitwise_xor(lead_irrep[:, None], irrep[None, :]) + 8 * (
        lead_spin[:, None] + spin[None, :]
    )


def dense(amplitudes, integrals, irrep, spin):
    virtuals = irrep.shape[0]
    a_count = integrals.shape[0] // virtuals
    c_count = integrals.shape[1] // virtuals
    col = ("plane", "sub")

    def labels(first, count):
        return pair_labels(
            lax.dynamic_slice_in_dim(irrep, first, count, 0),
            lax.dynamic_slice_in_dim(spin, first, count, 0),
            irrep,
            spin,
        ).reshape(-1)

    ab_labels = labels(lax.axis_index(col) * a_count, a_count)
    cd_labels = labels(lax.axis_index("row") * c_count, c_count)
    masked = jnp.where(
        ab_labels[:, None] == cd_labels[None, :], integrals, jnp.zeros((), integrals.dtype)
    )
    grid_rows = lax.all_gather(amplitudes, col, axis=0, tiled=True)
    regrouped = lax.all_to_all(grid_rows, "row", split_axis=1, concat_axis=0, tiled=True)
    partial_sums = lax.dot_general(regrouped, masked, NT, preferred_element_type=jnp.float32)
    return lax.psum_scatter(partial_sums, "row", scatter_dimension=0, tiled=True).astype(
        jnp.bfloat16
    )


def pack_integrals_kernel(c_count, cap, row_label, cd_label, column_slot, row_slot, v_ref, out_ref):
    virtuals = v_ref.shape[0]
    front = None
    for c in range(c_count):
        block = v_ref[:, c * virtuals : (c + 1) * virtuals]
        keep = row_label[...] == cd_label[c : c + 1, :]
        masked = jnp.where(keep, block, jnp.zeros((), block.dtype))
        lane = lax.broadcasted_iota(jnp.int32, (virtuals, 384), 1)
        lane = jnp.where(lane >= 320, lane - 64, lane)
        place = (column_slot[:, c : c + 1] == lane).astype(jnp.bfloat16)
        term = jnp.dot(masked, place, preferred_element_type=jnp.float32)
        front = term if front is None else front + term
    front = front.astype(jnp.bfloat16)
    half = cap // 2
    for g in range(IRREPS):
        spot = lax.broadcasted_iota(jnp.int32, (cap, virtuals), 0) + g * cap
        rows = (row_slot[...] == spot).astype(jnp.bfloat16)
        packed = jnp.dot(rows, front, preferred_element_type=jnp.float32)
        left = lax.broadcasted_iota(jnp.int32, (half, LANES), 1) < 64
        tail = jnp.where(left, packed[:half, 256:], packed[half:, 256:])
        out_ref[g, :cap, :] = packed[:, :128].astype(jnp.bfloat16)
        out_ref[g, cap : 2 * cap, :] = packed[:, 128:256].astype(jnp.bfloat16)
        out_ref[g, 2 * cap :, :] = tail.astype(jnp.bfloat16)


def pack_amplitudes_kernel(c_total, cap, lead_irrep, slot, t_ref, out_ref, stacked, moved):
    pairs = t_ref.shape[0]
    virtuals = slot.shape[1]
    fold = LANES // pairs
    tiles = c_total // fold
    for j in range(tiles):
        for h in range(fold):
            c = h * tiles + j
            at = (j * fold + h) * pairs
            stacked[at : at + pairs, :] = t_ref[:, c * virtuals : (c + 1) * virtuals]
    for g in range(IRREPS):
        spot = lax.broadcasted_iota(jnp.int32, (cap, virtuals), 0) + g * cap
        rows = (slot[...] == spot).astype(jnp.bfloat16)
        moved[g] = lax.dot_general(
            rows, stacked[...], NT, preferred_element_type=jnp.float32
        ).astype(jnp.bfloat16)
    share = lax.broadcasted_iota(jnp.int32, (cap, LANES), 1) // pairs
    for g in range(IRREPS):
        for j in range(tiles):
            tile = None
            for h in range(fold):
                source = jnp.bitwise_xor(lead_irrep[h * tiles + j], g)
                part = moved[source, :, j * LANES : (j + 1) * LANES]
                tile = part if tile is None else jnp.where(share == h, part, tile)
            out_ref[g, j * cap : (j + 1) * cap, :] = tile


def contract_kernel(rows, subs, cap, lead_spin, low, target, t_ref, v_ref, out_ref, t_label, v_rows):
    plane = pl.program_id(0)
    half = cap // 2
    main = rows * 256
    wide = t_ref.shape[0] // rows

    @pl.when(plane == 0)
    def _():
        for s in range(3):
            for r in range(rows):
                spot = lax.broadcasted_iota(jnp.int32, (384, wide), 0)
                spot = jnp.where(spot >= 320, spot - 64, spot)
                place = (target[s * rows + r : s * rows + r + 1, :] == spot).astype(jnp.bfloat16)
                part = jnp.dot(
                    place, t_ref[r * wide : (r + 1) * wide, :], preferred_element_type=jnp.float32
                ).astype(jnp.bfloat16)
                t_label[s, r * 256 : (r + 1) * 256, :] = part[:256]
                t_label[s, main + r * 128 : main + (r + 1) * 128, :] = part[256:]

    for y in range(subs):
        for r in range(rows):
            source = r * subs + y
            v_rows[:, r * 256 : r * 256 + 128] = v_ref[0, source, :cap, :]
            v_rows[:, r * 256 + 128 : (r + 1) * 256] = v_ref[0, source, cap : 2 * cap, :]
            tail = v_ref[0, source, 2 * cap :, :]
            left = lax.broadcasted_iota(jnp.int32, (half, LANES), 1) < 64
            none = jnp.zeros((), tail.dtype)
            at = main + r * 128
            v_rows[:half, at : at + 128] = jnp.where(left, tail, none)
            v_rows[half:, at : at + 128] = jnp.where(left, none, tail)
        a = plane * subs + y
        s = lead_spin[a]
        first = jnp.dot(v_rows[...], t_label[s], preferred_element_type=jnp.float32)
        second = jnp.dot(v_rows[...], t_label[s + 1], preferred_element_type=jnp.float32)
        upper = lax.broadcasted_iota(jnp.int32, first.shape, 0) < low[a]
        result = jnp.where(upper, first, second).astype(jnp.bfloat16)
        pairs = result.shape[1] // rows
        for r in range(rows):
            out_ref[r, 0, y] = result[:, r * pairs : (r + 1) * pairs]


def in_vmem(limit=48):
    return pltpu.CompilerParams(vmem_limit_bytes=limit * 2**20)


VMEM = pl.BlockSpec(memory_space=pltpu.VMEM)
SMEM = pl.BlockSpec(memory_space=pltpu.SMEM)


def packed(rows, planes, subs, amplitudes, integrals, irrep, spin, ranks, counts, offsets):
    virtuals = irrep.shape[0]
    c_count = integrals.shape[1] // virtuals
    c_total = amplitudes.shape[1] // virtuals
    a_total = planes * subs
    pairs = amplitudes.shape[0]
    cap = virtuals // IRREPS * 5 // 4
    row, plane, sub = (lax.axis_index(n) for n in ("row", "plane", "sub"))
    mine = row * subs + sub
    a = plane * subs + sub
    a_irrep = lax.dynamic_index_in_dim(irrep, a, keepdims=False)
    a_spin = lax.dynamic_index_in_dim(spin, a, keepdims=False)

    row_label = jnp.bitwise_xor(a_irrep, irrep) + 8 * (a_spin + spin)
    cd_label = pair_labels(
        lax.dynamic_slice_in_dim(irrep, row * c_count, c_count),
        lax.dynamic_slice_in_dim(spin, row * c_count, c_count),
        irrep,
        spin,
    )
    my_offsets = lax.dynamic_index_in_dim(offsets, row, keepdims=False)
    labels = jnp.arange(24, dtype=jnp.int32)
    rank16 = ranks[0]
    column_slot = rank16[None, :] + jnp.sum(
        jnp.where(cd_label[:, :, None] == labels, my_offsets[:, None, :], 0), axis=2
    )
    row_slot = jnp.bitwise_xor(irrep, a_irrep) * cap + ranks[1]
    v_packed = pl.pallas_call(
        functools.partial(pack_integrals_kernel, c_count, cap),
        out_shape=jax.ShapeDtypeStruct((IRREPS, cap * 5 // 2, LANES), jnp.bfloat16),
        in_specs=[VMEM] * 5,
        out_specs=VMEM,
        compiler_params=in_vmem(),
        name="pack_integrals",
    )(row_label[:, None], cd_label, column_slot.T, row_slot[None, :], integrals)
    v_plane = lax.all_to_all(v_packed, ("row", "sub"), 0, 0, tiled=True)
    v_all = lax.all_gather(v_plane, "plane", axis=0)

    fold = LANES // pairs
    tiles = c_total // fold
    t_slot = irrep * cap + ranks[1]
    t_packed = pl.pallas_call(
        functools.partial(pack_amplitudes_kernel, c_total, cap),
        out_shape=jax.ShapeDtypeStruct((IRREPS, tiles * cap, LANES), jnp.bfloat16),
        in_specs=[SMEM, VMEM, VMEM],
        out_specs=VMEM,
        scratch_shapes=[
            pltpu.VMEM((c_total * pairs, virtuals), jnp.bfloat16),
            pltpu.VMEM((IRREPS, cap, c_total * pairs), jnp.bfloat16),
        ],
        compiler_params=in_vmem(),
        name="pack_amplitudes",
    )(irrep[:c_total], t_slot[None, :], amplitudes)
    t_mine = lax.all_to_all(t_packed, ("row", "sub"), 0, 0, tiled=True)
    t_mine = t_mine.reshape(rows, subs, tiles, cap, fold, pairs).transpose(4, 2, 3, 0, 1, 5)
    group = rows * subs * pairs
    t_mine = t_mine.reshape(c_total * cap, group)

    lead_irrep = jnp.bitwise_xor(irrep[:c_total], mine)
    lead_spin = spin[:c_total]
    irreps = jnp.arange(IRREPS, dtype=jnp.int32)
    lows = jnp.sum(jnp.where(lead_irrep[:, None] == irreps, counts[None, :IRREPS], 0), axis=1)
    highs = jnp.sum(jnp.where(lead_irrep[:, None] == irreps, counts[None, IRREPS:], 0), axis=1)
    sums = jnp.arange(3, dtype=jnp.int32)[:, None]
    spins = sums - lead_spin[None, :]
    shift = jnp.sum(
        jnp.where(
            labels[None, None, :] == (mine + 8 * sums)[:, :, None],
            offsets.reshape(c_total, 24)[None],
            0,
        ),
        axis=2,
    )
    least = jnp.where(spins == 1, lows, 0)
    most = jnp.where(spins == 0, lows, jnp.where(spins == 1, lows + highs, 0))
    place = jnp.arange(cap, dtype=jnp.int32)
    target = jnp.where(
        (place >= least[..., None]) & (place < most[..., None]),
        place + (shift - least)[..., None],
        -1,
    ).reshape(3 * rows, c_count * cap)
    first_irrep = jnp.bitwise_xor(irrep[:a_total], mine)
    first_low = jnp.sum(
        jnp.where(first_irrep[:, None] == irreps, counts[None, :IRREPS], 0), axis=1
    )
    result = pl.pallas_call(
        functools.partial(contract_kernel, rows, subs, cap),
        out_shape=jax.ShapeDtypeStruct((rows, planes, subs, cap, group // rows), jnp.bfloat16),
        grid=(planes,),
        in_specs=[
            SMEM,
            SMEM,
            pl.BlockSpec((3 * rows, c_count * cap), lambda z: (0, 0)),
            pl.BlockSpec((c_total * cap, group), lambda z: (0, 0)),
            pl.BlockSpec((1, rows * subs, cap * 5 // 2, LANES), lambda z: (z, 0, 0, 0)),
        ],
        out_specs=pl.BlockSpec(
            (rows, 1, subs, cap, group // rows), lambda z: (0, z, 0, 0, 0)
        ),
        scratch_shapes=[
            pltpu.VMEM((3, rows * 384, group), jnp.bfloat16),
            pltpu.VMEM((cap, rows * 384), jnp.bfloat16),
        ],
        compiler_params=in_vmem(),
        name="contract",
    )(spin[:a_total], first_low, target, t_mine, v_all)
    result = result.reshape(rows * planes * subs, cap, group // rows)
    back = lax.all_to_all(result, ("row", "plane", "sub"), 0, 0, tiled=True)
    back = back.reshape(rows, planes, subs, cap, group // rows)
    spots = jnp.arange(IRREPS * cap, dtype=jnp.int32)
    rows_back = (spots[:, None] == row_slot[None, :]).astype(jnp.bfloat16)
    out = lax.dot_general(
        back,
        rows_back.reshape(rows, subs, cap, virtuals),
        (((0, 2, 3), (0, 1, 2)), ((), ())),
        preferred_element_type=jnp.float32,
    )
    return out.reshape(planes * group // rows, virtuals).astype(jnp.bfloat16)


def local(rows, planes, subs, amplitudes, integrals, irrep, spin):
    virtuals = irrep.shape[0]
    c_count = integrals.shape[1] // virtuals
    c_total = amplitudes.shape[1] // virtuals
    kind = irrep + IRREPS * spin
    hot = (kind[:, None] == jnp.arange(2 * IRREPS, dtype=jnp.int32)).astype(jnp.bfloat16)
    upto = jnp.tril(jnp.ones((virtuals, virtuals), jnp.bfloat16))
    running = jnp.dot(upto, hot, preferred_element_type=jnp.float32)
    counts = running[-1].astype(jnp.int32)
    running = running.astype(jnp.int32)
    before = jnp.concatenate([jnp.zeros((IRREPS,), jnp.int32), counts[:IRREPS]])
    here = hot > 0
    ranks = jnp.stack(
        [
            jnp.sum(jnp.where(here, running, 0), axis=1) - 1,
            jnp.sum(jnp.where(here, running + before, 0), axis=1) - 1,
        ]
    )
    labels = jnp.arange(24, dtype=jnp.int32)
    d_irrep = jnp.bitwise_xor(irrep[:c_total, None], labels % IRREPS)
    d_spin = labels // IRREPS - spin[:c_total, None]
    kinds = jnp.arange(2 * IRREPS, dtype=jnp.int32)
    found = (d_irrep[..., None] == kinds % IRREPS) & (d_spin[..., None] == kinds // IRREPS)
    sizes = jnp.sum(jnp.where(found, counts, 0), axis=2).reshape(rows, c_count, 24)
    order = jnp.arange(c_count)
    earlier = order[None, :] < order[:, None]
    offsets = jnp.sum(jnp.where(earlier[None, :, :, None], sizes[:, None], 0), axis=2)
    fits = (jnp.max(counts[:IRREPS] + counts[IRREPS:]) <= virtuals // IRREPS * 5 // 4) & (
        jnp.max(jnp.sum(sizes, axis=1)) <= c_count * virtuals // 16 * 5 // 4
    )
    return lax.cond(
        fits,
        lambda: packed(
            rows, planes, subs, amplitudes, integrals, irrep, spin, ranks, counts, offsets
        ),
        lambda: dense(amplitudes, integrals, irrep, spin),
    )


def solution(mesh):
    rows, cols = mesh.shape["row"], mesh.shape["col"]
    subs = IRREPS // rows
    planes = cols // subs
    split = Mesh(mesh.devices.reshape(rows, planes, subs), ("row", "plane", "sub"))
    col = ("plane", "sub")
    placed = (P(("row",) + col, None), P(col, "row"), P(), P())
    return jax.shard_map(
        functools.partial(local, rows, planes, subs),
        mesh=split,
        in_specs=placed,
        out_specs=P("row", col),
        check_vma=False,
    )
```

time: 578 us -> 190 us (0.33)
  waiting for transfers between devices: 483 us -> 61.5 us
  Pallas kernels: 0 us -> 28.2 us
  matrix products: 24.2 us -> 3.13 us
  blocking collectives: 0 us -> 17.8 us
    all_gather x1, waiting for transfers between devices: 233 us -> 0.02 us  [packed(): v_all = lax.all_gather(v_plane, 'plane', axis=0)]
    all_to_all x1 -> x2, waiting for transfers between devices: 180 us -> 61.4 us  [the longest x1 33.2 us: packed(): back = lax.all_to_all(result, ('row', 'plane', 'sub'), 0, 0, tiled=True)]
    reduce_scatter x1 -> x0, waiting for transfers between devices: 69.2 us -> none  [local(): lax.psum_scatter(partial_sums, 'row', scatter_dimension=0, tiled=True)]
    reshape x0 -> x4, local copies, waits for them, and re-layouts: none -> 34.7 us  [the longest x2 25.4 us: packed(): t_mine = t_mine.reshape(c_total * cap, group)]
    pallas_call x0 -> x3, Pallas kernels: none -> 28.2 us  [the longest x1 10.2 us: packed(): pl.pallas_call(functools.partial(contract_kernel, rows, subs, cap), out_s...]
    all_gather x1 -> x0, local copies, waits for them, and re-layouts: 22.4 us -> none  [local(): grid_rows = lax.all_gather(amplitudes, 'col', axis=0, tiled=True)]
    dot_general x1 -> x2, matrix products: 24.2 us -> 3.13 us  [the longest x1 2.66 us: packed(): lax.dot_general(back, rows_back.reshape(rows, subs, cap, virtuals), (((0,...]
    all_to_all x1, local copies, waits for them, and re-layouts: 20.7 us -> 2.58 us  [packed(): t_mine = lax.all_to_all(t_packed, ('row', 'sub'), 0, 0, tiled=True)]
  transfers between devices with their start and end apart: 3 -> 3, of which waited for: 3 -> 2; matrix products, arithmetic and copies ran while one was open for 0% -> 21% of each run, Pallas kernels for 0% -> 4%
where the time goes in v1:
time: 190 us; the launch traced here: 189 us
  waiting for transfers between devices  61.5 us (32%)
  local copies, waits for them, and re-layouts  46.5 us (24%)
  Pallas kernels  28.2 us (15%)
  blocking collectives  17.8 us (9%)
  between operations  14.7 us (8%)
  starting transfers between devices  8.92 us (5%)
  other arithmetic  7.73 us (4%)
  matrix products  3.13 us (2%)
    all_to_all x1, waiting for transfers between devices, packed(): back = lax.all_to_all(result, ('row', 'plane', 'sub'), 0, 0, tiled=True)  33.2 us
    all_to_all x1, waiting for transfers between devices, packed(): t_mine = lax.all_to_all(t_packed, ('row', 'sub'), 0, 0, tiled=True)  28.3 us
    reshape x2, local copies, waits for them, and re-layouts, packed(): t_mine = t_mine.reshape(c_total * cap, group)  25.4 us
    all_to_all x1, blocking collectives, packed(): v_plane = lax.all_to_all(v_packed, ('row', 'sub'), 0, 0, tiled=True)  17.8 us
    pallas_call x1, Pallas kernels, packed(): pl.pallas_call(functools.partial(contract_kernel, rows, subs, cap), out_s...  10.2 us
    pallas_call x1, Pallas kernels, packed(): pl.pallas_call(functools.partial(pack_integrals_kernel, c_count, cap), ou...  9.49 us
    pallas_call x1, Pallas kernels, packed(): pl.pallas_call(functools.partial(pack_amplitudes_kernel, c_total, cap), o...  8.49 us
    reshape x1, local copies, waits for them, and re-layouts, packed(): t_mine.reshape(rows, subs, tiles, cap, fold, pairs)  8.28 us
  transfers between devices with their start and end apart: 3, of which 2 were waited for; matrix products, arithmetic and copies ran while one was open for 21% of the time, Pallas kernels for 4%

profile of v1, /device:TPU:0, one launch (start us, length us, event | category | flops | bytes accessed | tf_op | source)
XLA Modules:
  0.0 188.8 jit_solution(16694956848562640781)
XLA Ops:
  6.5 0.7 multiply_add_fusion.7
  8.0 0.6 add_reduce_fusion
  9.4 0.7 slice.48
  10.1 0.7 slice.47
  11.0 0.6 reduce_max.19
  12.4 169.5 %conditional.6 = (bf16[512,1024]{1,0:T(8,128)(2,1)}) conditional(s32[]{:T(128)} %convert_element_type.30, (s32[1024]{0:T(1024)}, s32[1024]{0:T(1024)}, bf16[1024,4096]{1,0:T(8,128)(2,1)}, bf16[64,16384]{1,0:T(8,128)(2,1)}) %tuple.21, (s32[1024]{0:T(1024)}, s32[1024]{0:T(1024)}, s32[16]{0:T(128)S(1)}, s32[4,4]{1,0:T(4,128)S(1)}, ...), branch_computations={%region_7.9_spmd, %region_9.15_spmd} | conditional | flops 17188802560 | bytes 244441664
  12.7 1.3 dynamic_slice.24
  13.9 1.3 dynamic_slice.25
  15.3 0.8 dynamic_slice.27
  16.1 0.8 dynamic_slice.26
  17.0 2.0 %multiply_add_fusion.3 = (s32[1024]{0:T(1024)S(1)}, s32[1024]{0:T(1024)S(1)}, s32[1024]{0:T(1024)S(1)}, s32[1024]{0:T(1024)S(1)}) fusion(s32[1024]{0:T(1024)} %get-tuple-element.43, s32[]{:T(128)} %bitcast.9, s32[1024]{0:T(1024)S(1)} %get-tuple-element.92, s32[1024]{0:T(1024)S(1)} %get-tuple-element.137, s32[1024]{0:T(1024)S(1)} %get-tuple-element.91, ...), kind=kLoop, calls=%fused_computation.30 | loop fusion | flops 10240 | bytes 36872 | tf_op jit(solution)/shard_map/cond/branch_1_fun/add | solution.py:175
  19.3 0.8 multiply_add_fusion.1.cd_label
  20.6 9.5 %pack_integrals.1 = bf16[8,400,128]{2,1,0:T(8,128)(2,1)S(1)} custom-call(s32[1024,1]{1,0:T(8,128)S(1)} %copy.48.row_label, s32[4,1024]{1,0:T(4,128)S(1)} %multiply_add_fusion.1.cd_label, s32[1024,4]{1,0:T(8,128)S(1)} %bitcast.40, s32[1,1024]{1,0:T(1,128)S(1)} %bitcast.41, bf16[1024,4096]{1,0:T(8,128)(2,1)} %get-tuple-element.49.v_ref), custom_call_target="tpu_custom_call" | custom-call | tf_op jit(solution)/shard_map/cond/branch_1_fun/pack_integrals/pallas_call | solution.py:176
  30.1 17.8 %all_to_all.27 = bf16[8,400,128]{2,1,0:T(8,128)(2,1)} all-to-all(bf16[8,400,128]{2,1,0:T(8,128)(2,1)S(1)} %pack_integrals.1), channel_id=1, replica_groups=mesh['row'=4,'plane'=4,'sub'=2] {'row','sub'}, dimensions={0} | all-to-all | bytes 1638400 | tf_op jit(solution)/shard_map/cond/branch_1_fun/all_to_all | solution.py:184
  48.0 0.7 fusion.29
  48.7 8.5 %pack_amplitudes.1 = bf16[8,1280,128]{2,1,0:T(8,128)(2,1)} custom-call(s32[16]{0:T(128)S(1)} %get-tuple-element.101.lead_irrep, s32[1,1024]{1,0:T(1,128)S(1)} %bitcast.42, bf16[64,16384]{1,0:T(8,128)(2,1)S(1)} %copy-done.1), custom_call_target="tpu_custom_call" | custom-call | tf_op jit(solution)/shard_map/cond/branch_1_fun/pack_amplitudes/pallas_call | solution.py:190
  57.1 3.8 %all-to-all-start = ((bf16[8,1280,128]{2,1,0:T(8,128)(2,1)}), bf16[8,1280,128]{2,1,0:T(8,128)(2,1)S(1)}, u32[]{:S(2)}, u32[]{:S(2)}) async-start(bf16[8,1280,128]{2,1,0:T(8,128)(2,1)} %pack_amplitudes.1), calls=%async_computation | async-start | bytes 5242880 | tf_op jit(solution)/shard_map/cond/branch_1_fun/all_to_all | solution.py:202
  61.0 0.7 slice.29.lead_spin
  61.7 0.7 slice.32
  62.4 0.8 fusion.30
  63.8 28.3 %all-to-all-done = bf16[8,1280,128]{2,1,0:T(8,128)(2,1)S(1)} async-done(((bf16[8,1280,128]{2,1,0:T(8,128)(2,1)}), bf16[8,1280,128]{2,1,0:T(8,128)(2,1)S(1)}, u32[]{:S(2)}, u32[]{:S(2)}) %all-to-all-start) | async-done | bytes 2621472 | tf_op jit(solution)/shard_map/cond/branch_1_fun/all_to_all | solution.py:202
  92.1 2.6 %copy.45 = bf16[8,1280,128]{1,2,0:T(8,128)(2,1)} copy(bf16[8,1280,128]{2,1,0:T(8,128)(2,1)S(1)} %all-to-all-done) | data formatting | bytes 5242880 | tf_op jit(solution)/shard_map/cond/branch_1_fun/all_to_all | solution.py:202
  94.7 8.3 %reshape.410 = bf16[4,2,8,160,2,64]{3,2,5,4,1,0:T(8,128)(2,1)} reshape(bf16[8,1280,128]{1,2,0:T(8,128)(2,1)} %copy.45) | data formatting | bytes 5242880 | tf_op jit(solution)/shard_map/cond/branch_1_fun/reshape | solution.py:203
  103.0 14.0 %copy.52 = bf16[2,8,160,4,2,64]{5,4,3,2,1,0:T(2,128)(2,1)} copy(bf16[2,8,160,4,2,64]{2,1,5,0,4,3:T(8,128)(2,1)} %bitcast.45) | data formatting | bytes 5242880 | tf_op jit(solution)/shard_map/cond/branch_1_fun/reshape | solution.py:205
  116.9 11.4 %reshape.419.t_ref = bf16[2560,512]{1,0:T(8,128)(2,1)S(1)} reshape(bf16[2,8,160,4,2,64]{5,4,3,2,1,0:T(2,128)(2,1)} %copy.52) | data formatting | bytes 5242880 | tf_op jit(solution)/shard_map/cond/branch_1_fun/reshape | solution.py:205
  128.4 10.2 %contract.1 = bf16[4,4,2,160,128]{4,3,2,1,0:T(8,128)(2,1)S(1)} custom-call(s32[8]{0:T(128)S(1)} %slice.29.lead_spin, s32[8]{0:T(128)S(1)} %select_reduce_fusion.6.low, s32[12,640]{1,0:T(8,128)S(1)} %select_n.122.target, bf16[2560,512]{1,0:T(8,128)(2,1)S(1)} %reshape.419.t_ref, bf16[4,8,400,128]{3,2,1,0:T(8,128)(2,1)} %bitcast.48), custom_call_target="tpu_custom_call" | custom-call | tf_op jit(solution)/shard_map/cond/branch_1_fun/contract/pallas_call | solution.py:234
  138.6 1.1 copy-done
  139.7 4.9 %all-to-all-start.2 = ((bf16[32,160,128]{2,1,0:T(8,128)(2,1)}), bf16[32,160,128]{2,1,0:T(8,128)(2,1)S(1)}, u32[]{:S(2)}, u32[]{:S(2)}) async-start(bf16[32,160,128]{2,1,0:T(8,128)(2,1)} %bitcast.39), calls=%async_computation.2 | async-start | bytes 2621440 | tf_op jit(solution)/shard_map/cond/branch_1_fun/all_to_all | solution.py:256
  144.5 33.2 %all-to-all-done.2 = bf16[32,160,128]{2,1,0:T(8,128)(2,1)S(1)} async-done(((bf16[32,160,128]{2,1,0:T(8,128)(2,1)}), bf16[32,160,128]{2,1,0:T(8,128)(2,1)S(1)}, u32[]{:S(2)}, u32[]{:S(2)}) %all-to-all-start.2) | async-done | bytes 1310752 | tf_op jit(solution)/shard_map/cond/branch_1_fun/all_to_all | solution.py:256
  177.7 1.0 copy.57
  178.8 0.5 dot_general.12
  179.3 2.7 %bitcast_convert_fusion = bf16[512,1024]{1,0:T(8,128)(2,1)} fusion(bf16[512,4,2,160]{0,3,2,1:T(8,128)(2,1)S(1)} %dot_general.12, s32[1024]{0:T(1024)S(1)} %get-tuple-element.97, s32[4,2,160]{2,1,0:T(2,128)S(1)} %multiply_add_fusion.2), kind=kOutput, calls=%fused_computation.14 | convolution fusion | flops 1344012288 | bytes 2368512 | tf_op jit(solution)/shard_map/cond/branch_1_fun/dot_general | solution.py:260
  (40 shorter events, 3.0 us)
Async XLA Ops:
  12.4 115.9 %all-gather.6.cloned.1.call-start = ((), (), s32[]{:S(2)}) async-start(), calls=%async_computation.7 | async-start | bytes 4096000 | tf_op jit(solution)/shard_map/cond/branch_1_fun/all_gather | solution.py:185
  20.6 28.1 %copy-start.1 = (bf16[64,16384]{1,0:T(8,128)(2,1)S(1)}, bf16[64,16384]{1,0:T(8,128)(2,1)}, u32[]{:S(2)}) copy-start(bf16[64,16384]{1,0:T(8,128)(2,1)} %get-tuple-element.47.t_ref) | copy-start | bytes 6291460 | tf_op jit(solution)/shard_map/conditional.1
  57.1 35.0 %all-to-all-start = ((bf16[8,1280,128]{2,1,0:T(8,128)(2,1)}), bf16[8,1280,128]{2,1,0:T(8,128)(2,1)S(1)}, u32[]{:S(2)}, u32[]{:S(2)}) async-start(bf16[8,1280,128]{2,1,0:T(8,128)(2,1)} %pack_amplitudes.1), calls=%async_computation | async-start | bytes 5242880 | tf_op jit(solution)/shard_map/cond/branch_1_fun/all_to_all | solution.py:202
  138.6 1.1 copy-start
  139.7 38.1 %all-to-all-start.2 = ((bf16[32,160,128]{2,1,0:T(8,128)(2,1)}), bf16[32,160,128]{2,1,0:T(8,128)(2,1)S(1)}, u32[]{:S(2)}, u32[]{:S(2)}) async-start(bf16[32,160,128]{2,1,0:T(8,128)(2,1)} %bitcast.39), calls=%async_computation.2 | async-start | bytes 2621440 | tf_op jit(solution)/shard_map/cond/branch_1_fun/all_to_all | solution.py:256
Sparse Core Ops, SparseCore 0:
  48.1 65.1 all-gather.5

commit v2 on v0

v2 whole, which is shorter than its diff:
```python
import functools

import jax
import jax.numpy as jnp
from jax import lax
from jax.experimental import pallas as pl
from jax.experimental.pallas import tpu as pltpu
from jax.sharding import Mesh, PartitionSpec as P

IRREPS = 8
LANES = 128
NT = (((1,), (1,)), ((), ()))


def pair_labels(lead_irrep, lead_spin, irrep, spin):
    return jnp.bitwise_xor(lead_irrep[:, None], irrep[None, :]) + 8 * (
        lead_spin[:, None] + spin[None, :]
    )


def dense(rows, cols, amplitudes, integrals, irrep, spin):
    virtuals = irrep.shape[0]
    a_count = integrals.shape[0] // virtuals
    c_count = integrals.shape[1] // virtuals
    pairs = amplitudes.shape[0]
    col = ("plane", "sub")

    def labels(first, count):
        return pair_labels(
            lax.dynamic_slice_in_dim(irrep, first, count, 0),
            lax.dynamic_slice_in_dim(spin, first, count, 0),
            irrep,
            spin,
        ).reshape(-1)

    ab_labels = labels(lax.axis_index(col) * a_count, a_count)
    cd_labels = labels(lax.axis_index("row") * c_count, c_count)
    masked = jnp.where(
        ab_labels[:, None] == cd_labels[None, :], integrals, jnp.zeros((), integrals.dtype)
    )
    mine = lax.all_to_all(amplitudes, "row", split_axis=1, concat_axis=0, tiled=True)
    copies = jnp.broadcast_to(mine[None], (cols,) + mine.shape)
    regrouped = lax.all_to_all(copies, col, 0, 0, tiled=True)
    partial_sums = lax.dot_general(
        regrouped.reshape(-1, mine.shape[1]), masked, NT, preferred_element_type=jnp.float32
    )
    partial_sums = partial_sums.reshape(cols, rows, pairs, -1).transpose(1, 0, 2, 3)
    parts = lax.all_to_all(partial_sums, "row", 0, 0, tiled=True)
    return jnp.sum(parts, axis=0).reshape(cols * pairs, -1).astype(jnp.bfloat16)


def pack_integrals_kernel(
    c_count, c_total, subs, cap, label_cap, irrep_s, spin_s, irrep_v, spin_v, v_hbm, *refs
):
    out, slots_out, offsets_out, counts_out, fits_out, v_ref, arrived = refs
    virtuals = v_ref.shape[1]
    copies = []
    for i in range(c_count):
        copies.append(
            pltpu.make_async_copy(
                v_hbm.at[:, i * virtuals : (i + 1) * virtuals], v_ref.at[i], arrived.at[i]
            )
        )
        copies[-1].start()
    row = lax.axis_index("row")
    a = lax.axis_index("plane") * subs + lax.axis_index("sub")
    irrep, spin = irrep_v[...], spin_v[...]
    kinds = 2 * IRREPS
    kind = irrep + IRREPS * spin
    hot = lax.broadcasted_iota(jnp.int32, (kinds, virtuals), 0) == kind
    shape = (virtuals, virtuals)
    upto = lax.broadcasted_iota(jnp.int32, shape, 0) <= lax.broadcasted_iota(jnp.int32, shape, 1)
    blocks = virtuals // LANES
    shape = (LANES, LANES)
    upto = lax.broadcasted_iota(jnp.int32, shape, 0) <= lax.broadcasted_iota(jnp.int32, shape, 1)
    ones = jnp.where(hot, 1.0, 0.0)
    stacked = jnp.concatenate(
        [ones[:, k * LANES : (k + 1) * LANES] for k in range(blocks)], axis=0
    )
    inside = jnp.dot(
        stacked.astype(jnp.bfloat16),
        jnp.where(upto, 1.0, 0.0).astype(jnp.bfloat16),
        preferred_element_type=jnp.float32,
    ).astype(jnp.int32)
    counts = jnp.zeros((kinds, LANES), jnp.int32)
    running = []
    for k in range(blocks):
        block = inside[k * kinds : (k + 1) * kinds] + counts
        running.append(block)
        counts = jnp.broadcast_to(block[:, LANES - 1 :], (kinds, LANES))
    running = jnp.concatenate(running, axis=1)
    counts_out[...] = counts
    rank16 = jnp.sum(jnp.where(hot, running, 0), axis=0, keepdims=True) - 1
    before = jnp.sum(
        jnp.where(hot[IRREPS:], counts[:IRREPS, :1], 0), axis=0, keepdims=True
    )
    rank8 = rank16 + before

    which = lax.broadcasted_iota(jnp.int32, (c_total, LANES), 0)
    lead_irrep = jnp.zeros((c_total, LANES), jnp.int32)
    lead_spin = jnp.zeros((c_total, LANES), jnp.int32)
    for c in range(c_total):
        lead_irrep = jnp.where(which == c, irrep_s[c], lead_irrep)
        lead_spin = jnp.where(which == c, spin_s[c], lead_spin)
    label = lax.broadcasted_iota(jnp.int32, (c_total, LANES), 1)
    d_irrep = jnp.bitwise_xor(label & (IRREPS - 1), lead_irrep)
    d_spin = (label >> 3) - lead_spin
    d_kind = jnp.where((d_spin >= 0) & (d_spin <= 1), d_irrep + IRREPS * d_spin, -1)
    sizes = jnp.zeros((c_total, LANES), jnp.int32)
    for k in range(kinds):
        sizes = jnp.where(d_kind == k, counts[k : k + 1, :], sizes)
    within = lax.broadcasted_iota(jnp.int32, (c_total, LANES), 0) % c_count
    offsets = jnp.zeros((c_total, LANES), jnp.int32)
    for k in range(1, c_count):
        offsets += jnp.where(within >= k, pltpu.roll(sizes, k, 0), 0)
    offsets_out[...] = offsets
    irrep_most = jnp.max(counts[:IRREPS] + counts[IRREPS:])
    label_most = jnp.max(offsets + sizes)
    fits_out[0] = jnp.where((irrep_most <= cap) & (label_most <= label_cap), 1, 0)

    row_label = jnp.bitwise_xor(irrep, irrep_s[a]) + 8 * (spin + spin_s[a])
    row_slot = jnp.bitwise_xor(irrep, irrep_s[a]) * cap + rank8
    slots_out[0:1, :] = row_slot
    slots_out[1:2, :] = irrep * cap + rank8
    which = lax.broadcasted_iota(jnp.int32, (8, LANES), 0)
    first_irrep = jnp.zeros((8, LANES), jnp.int32)
    first_spin = jnp.zeros((8, LANES), jnp.int32)
    start = jnp.zeros((8, LANES), jnp.int32)
    for i in range(c_count):
        c = row * c_count + i
        first_irrep = jnp.where(which == i, irrep_s[c], first_irrep)
        first_spin = jnp.where(which == i, spin_s[c], first_spin)
        start = jnp.where(which == i, offsets_out[pl.ds(c, 1), :], start)
    cd_label = jnp.bitwise_xor(irrep, first_irrep[:, :1]) + 8 * (spin + first_spin[:, :1])
    lines = jnp.broadcast_to(rank16, (8, virtuals))
    for k in range(24):
        lines = lines + jnp.where(cd_label == k, start[:, k : k + 1], 0)
    lines = jnp.where(
        lax.broadcasted_iota(jnp.int32, (8, virtuals), 0) < c_count, lines, row_label
    )
    columns = lines.astype(jnp.float32).T.astype(jnp.int32)
    row_label = columns[:, c_count : c_count + 1]

    front = None
    for i in range(c_count):
        copies[i].wait()
        masked = jnp.where(
            row_label == cd_label[i : i + 1], v_ref[i], jnp.zeros((), v_ref.dtype)
        )
        lane = lax.broadcasted_iota(jnp.int32, (virtuals, 384), 1)
        lane = jnp.where(lane >= 320, lane - 64, lane)
        place = (columns[:, i : i + 1] == lane).astype(jnp.bfloat16)
        term = jnp.dot(masked, place, preferred_element_type=jnp.float32)
        front = term if front is None else front + term
    front = front.astype(jnp.bfloat16)
    for g in range(IRREPS):
        spot = lax.broadcasted_iota(jnp.int32, (cap, virtuals), 0) + g * cap
        rows = (row_slot == spot).astype(jnp.bfloat16)
        packed = jnp.dot(rows, front, preferred_element_type=jnp.float32)
        half = cap // 2
        left = lax.broadcasted_iota(jnp.int32, (half, LANES), 1) < 64
        tail = jnp.where(left, packed[:half, 256:], packed[half:, 256:])
        out[g, :cap, :] = packed[:, :128].astype(jnp.bfloat16)
        out[g, cap : 2 * cap, :] = packed[:, 128:256].astype(jnp.bfloat16)
        out[g, 2 * cap :, :] = tail.astype(jnp.bfloat16)


def pack_amplitudes_kernel(c_total, cap, irrep_s, slots, t_ref, out_ref, stacked, moved):
    pairs = t_ref.shape[0]
    virtuals = slots.shape[1]
    fold = LANES // pairs
    tiles = c_total // fold
    for j in range(tiles):
        for h in range(fold):
            c = h * tiles + j
            at = (j * fold + h) * pairs
            stacked[at : at + pairs, :] = t_ref[:, c * virtuals : (c + 1) * virtuals]
    for g in range(IRREPS):
        spot = lax.broadcasted_iota(jnp.int32, (cap, virtuals), 0) + g * cap
        rows = (slots[1:2, :] == spot).astype(jnp.bfloat16)
        moved[g] = lax.dot_general(
            rows, stacked[...], NT, preferred_element_type=jnp.float32
        ).astype(jnp.bfloat16)
    share = lax.broadcasted_iota(jnp.int32, (cap, LANES), 1) // pairs
    for g in range(IRREPS):
        for j in range(tiles):
            tile = None
            for h in range(fold):
                source = jnp.bitwise_xor(irrep_s[h * tiles + j], g)
                part = moved[source, :, j * LANES : (j + 1) * LANES]
                tile = part if tile is None else jnp.where(share == h, part, tile)
            out_ref[g, j * cap : (j + 1) * cap, :] = tile


def unpack_amplitudes_kernel(
    rows, subs, c_total, cap, pairs, irrep_s, spin_s, offsets, counts, t_ref, out_ref, quarter
):
    mine = lax.axis_index("row") * subs + lax.axis_index("sub")
    fold = LANES // pairs
    tiles = c_total // fold
    c_count = c_total // rows
    wide = c_count * cap
    group = out_ref.shape[2]
    main = rows * 256
    share = lax.broadcasted_iota(jnp.int32, (cap, LANES), 1) // pairs
    spot = lax.broadcasted_iota(jnp.int32, (384, wide), 0)
    spot = jnp.where(spot >= 320, spot - 64, spot)
    lane = lax.broadcasted_iota(jnp.int32, (1, wide), 1)
    for r in range(rows):
        for i in range(c_count):
            h, j = (r * c_count + i) // tiles, (r * c_count + i) % tiles
            for tile in range(group // LANES):
                whole = None
                for u in range(fold):
                    part = t_ref[tile * fold + u, j * cap : (j + 1) * cap, :]
                    if u != h:
                        part = pltpu.roll(
                            part.astype(jnp.float32), (u - h) * pairs % LANES, 1
                        ).astype(jnp.bfloat16)
                    whole = part if whole is None else jnp.where(share == u, part, whole)
                quarter[i * cap : (i + 1) * cap, tile * LANES : (tile + 1) * LANES] = whole
        for s in range(3):
            target = jnp.full((1, wide), -1, jnp.int32)
            for i in range(c_count):
                c = r * c_count + i
                irrep = jnp.bitwise_xor(irrep_s[c], mine)
                low, high = counts[irrep, 0], counts[irrep + IRREPS, 0]
                spin = s - spin_s[c]
                least = jnp.where(spin == 1, low, 0)
                most = jnp.where(spin == 0, low, jnp.where(spin == 1, low + high, 0))
                place = lane - i * cap
                inside = (place >= least) & (place < most) & (place >= 0) & (place < cap)
                start = offsets[c, mine + 8 * s]
                target = jnp.where(inside, place + (start - least), target)
            part = jnp.dot(
                (target == spot).astype(jnp.bfloat16),
                quarter[...],
                preferred_element_type=jnp.float32,
            ).astype(jnp.bfloat16)
            out_ref[s, r * 256 : (r + 1) * 256, :] = part[:256]
            out_ref[s, main + r * 128 : main + (r + 1) * 128, :] = part[256:]


def shift_of(k):
    return jnp.where(k % 2 == 1, -((k + 1) // 2), k // 2)


def contract_kernel(rows, planes, subs, first, last, irrep_s, spin_s, counts, t_ref, *refs):
    v_refs = refs[: last - first]
    if first:
        out_hbm, v_rows, sums, out_ref, copied = refs[-5:]
    else:
        out_ref, v_rows, sums = refs[-3:]
    plane = lax.axis_index("plane")
    mine = lax.axis_index("row") * subs + lax.axis_index("sub")
    n, pairs = out_ref.shape[3:]
    half = n // 2
    main = rows * 256
    left = lax.broadcasted_iota(jnp.int32, (half, LANES), 1) < 64
    for k, v_ref in enumerate(v_refs):
        for y in range(subs):
            top = y * n
            for r in range(rows):
                source = r * subs + y
                at = main + r * 128
                v_rows[k, top : top + n, r * 256 : r * 256 + 128] = v_ref[source, :n, :]
                v_rows[k, top : top + n, r * 256 + 128 : (r + 1) * 256] = v_ref[
                    source, n : 2 * n, :
                ]
                tail = v_ref[source, 2 * n :, :]
                none = jnp.zeros((), tail.dtype)
                v_rows[k, top : top + half, at : at + 128] = jnp.where(left, tail, none)
                v_rows[k, top + half : top + n, at : at + 128] = jnp.where(left, none, tail)
    slot = lax.broadcasted_iota(jnp.int32, (n, rows * pairs), 0)

    def one_plane(k, carry):
        for s in range(3):
            sums[s] = jnp.dot(v_rows[k], t_ref[s], preferred_element_type=jnp.float32)
        of = lax.rem(plane + shift_of(k + first) + planes, planes)
        for y in range(subs):
            a = of * subs + y
            s = spin_s[a]
            low = counts[jnp.bitwise_xor(irrep_s[a], mine), 0]
            lower = sums[s, y * n : (y + 1) * n, :]
            upper = sums[s + 1, y * n : (y + 1) * n, :]
            result = jnp.where(slot < low, lower, upper).astype(jnp.bfloat16)
            for r in range(rows):
                out_ref[r, k if first else of, y] = result[:, r * pairs : (r + 1) * pairs]
        return carry

    lax.fori_loop(0, last - first, one_plane, 0, unroll=last - first < 4)
    if first:
        for k in range(last - first):
            of = lax.rem(plane + shift_of(k + first) + planes, planes)
            copy = pltpu.make_async_copy(out_ref.at[:, k], out_hbm.at[:, of], copied)
            copy.start()
            copy.wait()


VMEM = pl.BlockSpec(memory_space=pltpu.VMEM)
SMEM = pl.BlockSpec(memory_space=pltpu.SMEM)
ANY = pl.BlockSpec(memory_space=pl.ANY)


def options(limit=24):
    return pltpu.CompilerParams(vmem_limit_bytes=limit * 2**20)


def cost(us):
    return pl.CostEstimate(flops=int(us * 1e9), bytes_accessed=0, transcendentals=0)


def ring_gather(block, planes):
    up = [(i, (i + 1) % planes) for i in range(planes)]
    down = [(i, (i - 1) % planes) for i in range(planes)]
    found = {0: block}
    for step in range(1, planes // 2 + 1):
        found[-step] = lax.ppermute(found[1 - step], "plane", up)
        if 2 * step < planes:
            found[step] = lax.ppermute(found[step - 1], "plane", down)
    return found


def packed(rows, planes, subs, amplitudes, irrep, spin, v_packed, slots, offsets, counts):
    virtuals = irrep.shape[0]
    pairs = amplitudes.shape[0]
    c_total = amplitudes.shape[1] // virtuals
    cap = virtuals // IRREPS * 5 // 4
    group = rows * subs * pairs
    tiles = c_total * pairs // LANES
    plane_axes, all_axes = ("row", "sub"), ("row", "plane", "sub")

    v_plane = lax.all_to_all(v_packed, plane_axes, 0, 0, tiled=True)
    found = ring_gather(v_plane, planes)
    t_packed = pl.pallas_call(
        functools.partial(pack_amplitudes_kernel, c_total, cap),
        out_shape=jax.ShapeDtypeStruct((IRREPS, tiles * cap, LANES), jnp.bfloat16),
        in_specs=[SMEM, VMEM, VMEM],
        out_specs=VMEM,
        scratch_shapes=[
            pltpu.VMEM((c_total * pairs, virtuals), jnp.bfloat16),
            pltpu.VMEM((IRREPS, cap, c_total * pairs), jnp.bfloat16),
        ],
        compiler_params=options(),
        cost_estimate=cost(8),
        name="pack_amplitudes",
    )(irrep, slots, amplitudes)
    t_mine = lax.all_to_all(t_packed, plane_axes, 0, 0, tiled=True)
    t_labels = pl.pallas_call(
        functools.partial(unpack_amplitudes_kernel, rows, subs, c_total, cap, pairs),
        out_shape=jax.ShapeDtypeStruct((3, rows * 384, group), jnp.bfloat16),
        in_specs=[SMEM] * 4 + [VMEM],
        out_specs=VMEM,
        scratch_shapes=[pltpu.VMEM((c_total // rows * cap, group), jnp.bfloat16)],
        compiler_params=options(),
        cost_estimate=cost(6),
        name="unpack_amplitudes",
    )(irrep, spin, offsets, counts, t_mine)

    shifts = sorted(found, key=abs)
    result = None
    for first, last in ((0, planes - 1), (planes - 1, planes)):
        shape = (rows, planes, subs, cap, group // rows)
        scratch = [
            pltpu.VMEM((last - first, subs * cap, rows * 384), jnp.bfloat16),
            pltpu.VMEM((3, subs * cap, group), jnp.float32),
        ]
        if first:
            scratch += [
                pltpu.VMEM((rows, last - first) + shape[2:], jnp.bfloat16),
                pltpu.SemaphoreType.DMA,
            ]
        blocks = [found[shift] for shift in shifts[first:last]]
        result = pl.pallas_call(
            functools.partial(contract_kernel, rows, planes, subs, first, last),
            out_shape=jax.ShapeDtypeStruct(shape, jnp.bfloat16),
            in_specs=[SMEM] * 3 + [VMEM] * (1 + len(blocks)) + [ANY] * bool(first),
            out_specs=ANY if first else VMEM,
            scratch_shapes=scratch,
            input_output_aliases={4 + len(blocks): 0} if first else {},
            compiler_params=options(),
            cost_estimate=cost(2 * len(blocks)),
            name="contract",
        )(irrep, spin, counts, t_labels, *blocks, *([result] if first else []))
    result = result.reshape(rows * planes * subs, cap, group // rows)
    back = lax.all_to_all(result, all_axes, 0, 0, tiled=True)
    back = back.reshape(rows, planes, subs, cap, group // rows)
    spots = jnp.arange(IRREPS * cap, dtype=jnp.int32)
    rows_back = (spots[:, None] == slots[0]).astype(jnp.bfloat16)
    out = lax.dot_general(
        back,
        rows_back.reshape(rows, subs, cap, virtuals),
        (((0, 2, 3), (0, 1, 2)), ((), ())),
        preferred_element_type=jnp.float32,
    )
    return out.reshape(planes * group // rows, virtuals).astype(jnp.bfloat16)


def local(rows, planes, subs, amplitudes, integrals, irrep, spin):
    virtuals = irrep.shape[0]
    c_count = integrals.shape[1] // virtuals
    c_total = amplitudes.shape[1] // virtuals
    cap = virtuals // IRREPS * 5 // 4
    label_cap = c_count * virtuals // (2 * IRREPS) * 5 // 4
    v_packed, slots, offsets, counts, fits = pl.pallas_call(
        functools.partial(
            pack_integrals_kernel, c_count, c_total, subs, cap, label_cap
        ),
        out_shape=[
            jax.ShapeDtypeStruct((IRREPS, cap * 5 // 2, LANES), jnp.bfloat16),
            jax.ShapeDtypeStruct((2, virtuals), jnp.int32),
            jax.ShapeDtypeStruct((c_total, LANES), jnp.int32),
            jax.ShapeDtypeStruct((2 * IRREPS, LANES), jnp.int32),
            jax.ShapeDtypeStruct((1,), jnp.int32),
        ],
        in_specs=[SMEM, SMEM, VMEM, VMEM, ANY],
        out_specs=[VMEM] * 4 + [SMEM],
        scratch_shapes=[
            pltpu.VMEM((c_count, virtuals, virtuals), jnp.bfloat16),
            pltpu.SemaphoreType.DMA((c_count,)),
        ],
        compiler_params=options(),
        cost_estimate=cost(9),
        name="pack_integrals",
    )(irrep, spin, irrep[None, :], spin[None, :], integrals)
    return lax.cond(
        fits[0] > 0,
        lambda: packed(
            rows, planes, subs, amplitudes, irrep, spin, v_packed, slots, offsets, counts
        ),
        lambda: dense(rows, planes * subs, amplitudes, integrals, irrep, spin),
    )


def solution(mesh):
    rows, cols = mesh.shape["row"], mesh.shape["col"]
    subs = IRREPS // rows
    planes = cols // subs
    split = Mesh(mesh.devices.reshape(rows, planes, subs), ("row", "plane", "sub"))
    col = ("plane", "sub")
    placed = (P(("row",) + col, None), P(col, "row"), P(), P())
    return jax.shard_map(
        functools.partial(local, rows, planes, subs),
        mesh=split,
        in_specs=placed,
        out_specs=P("row", col),
        check_vma=False,
    )
```

time: 578 us -> 136 us (0.24)
  waiting for transfers between devices: 483 us -> 78.3 us
  local copies, waits for them, and re-layouts: 45.7 us -> 3.06 us
  Pallas kernels: 0 us -> 33.9 us
  matrix products: 24.2 us -> 2.63 us
  between operations: 13.4 us -> 0.68 us
  starting transfers between devices: 7.15 us -> 16.8 us
    all_gather x1 -> x0, waiting for transfers between devices: 233 us -> none  [local(): grid_rows = lax.all_gather(amplitudes, 'col', axis=0, tiled=True)]
    all_to_all x1 -> x3, waiting for transfers between devices: 180 us -> 45 us  [the longest x1 33.2 us: packed(): back = lax.all_to_all(result, all_axes, 0, 0, tiled=True)]
    reduce_scatter x1 -> x0, waiting for transfers between devices: 69.2 us -> none  [local(): lax.psum_scatter(partial_sums, 'row', scatter_dimension=0, tiled=True)]
    pallas_call x0 -> x5, Pallas kernels: none -> 33.9 us  [the longest x1 11 us: local(): pl.pallas_call(functools.partial(pack_integrals_kernel, c_count, c_total,...]
    ppermute x0 -> x3, waiting for transfers between devices: none -> 33.3 us  [the longest x2 30 us: ring_gather(): found[-step] = lax.ppermute(found[1 - step], 'plane', up)]
    all_gather x1 -> x0, local copies, waits for them, and re-layouts: 22.4 us -> none  [local(): grid_rows = lax.all_gather(amplitudes, 'col', axis=0, tiled=True)]
    dot_general x1, matrix products: 24.2 us -> 2.63 us  [packed(): lax.dot_general(back, rows_back.reshape(rows, subs, cap, virtuals), (((0,...]
    all_to_all x1 -> x0, local copies, waits for them, and re-layouts: 20.7 us -> none  [local(): lax.all_to_all(grid_rows, 'row', split_axis=1, concat_axis=0, tiled=True)]
  transfers between devices with their start and end apart: 3 -> 6, of which waited for: 3 -> 6; matrix products, arithmetic and copies ran while one was open for 0% -> 0% of each run, Pallas kernels for 0% -> 14%
where the time goes in v2:
time: 136 us
  waiting for transfers between devices  78.3 us (58%)
  Pallas kernels  33.9 us (25%)
  starting transfers between devices  16.8 us (12%)
  local copies, waits for them, and re-layouts  3.06 us (2%)
  matrix products  2.63 us (2%)
    all_to_all x1, waiting for transfers between devices, packed(): back = lax.all_to_all(result, all_axes, 0, 0, tiled=True)  33.2 us
    ppermute x2, waiting for transfers between devices, ring_gather(): found[-step] = lax.ppermute(found[1 - step], 'plane', up)  30 us
    pallas_call x1, Pallas kernels, local(): pl.pallas_call(functools.partial(pack_integrals_kernel, c_count, c_total,...  11 us
    pallas_call x2, Pallas kernels, packed(): pl.pallas_call(functools.partial(contract_kernel, rows, planes, subs, fir...  10.9 us
    all_to_all x1, waiting for transfers between devices, packed(): t_mine = lax.all_to_all(t_packed, plane_axes, 0, 0, tiled=True)  8.25 us
    pallas_call x1, Pallas kernels, packed(): pl.pallas_call(functools.partial(pack_amplitudes_kernel, c_total, cap), o...  7.04 us
    all_to_all x1, starting transfers between devices, packed(): v_plane = lax.all_to_all(v_packed, plane_axes, 0, 0, tiled=True)  5.19 us
    pallas_call x1, Pallas kernels, packed(): pl.pallas_call(functools.partial(unpack_amplitudes_kernel, rows, subs, c_...  4.94 us
  transfers between devices with their start and end apart: 6, of which 6 were waited for; matrix products, arithmetic and copies ran while one was open for 0% of the time, Pallas kernels for 14%

profile of v2, /device:TPU:0, one launch (start us, length us, event | category | flops | bytes accessed | tf_op | source)
XLA Modules:
  0.0 135.7 jit_solution(14041154088277119321)
XLA Ops:
  0.0 0.0 copy-start.1
  0.0 0.0 copy-start.2
  0.0 0.0 copy-start.3
  0.0 11.0 %pack_integrals.1 = (bf16[8,400,128]{2,1,0:T(8,128)(2,1)}, s32[2,1024]{1,0:T(2,128)S(1)}, s32[16,128]{1,0:T(8,128)S(1)}, s32[16,128]{1,0:T(8,128)S(1)}, s32[1]{0:T(128)}) custom-call(s32[1024]{0:T(1024)} %irrep_s.1, s32[1024]{0:T(1024)} %spin_s.1, s32[1,1024]{1,0:T(1,128)} %bitcast.44, s32[1,1024]{1,0:T(1,128)} %bitcast.45, bf16[1024,4096]{1,0:T(8,128)(2,1)} %v_hbm.1), custom_call_target="tpu_custom_call" | custom-call | flops 8999999488 | tf_op jit(solution)/shard_map/pack_integrals/pallas_call | solution.py:405
  11.7 0.0 copy-done.1
  11.7 0.0 copy-done.2
  11.7 0.0 copy-done.3
  11.7 124.0 %conditional.6 = (bf16[512,1024]{1,0:T(8,128)(2,1)}) conditional(s32[]{:T(128)} %bitcast.17, (s32[1024]{0:T(1024)S(1)}, s32[1024]{0:T(1024)S(1)}, bf16[1024,4096]{1,0:T(8,128)(2,1)}, bf16[64,16384]{1,0:T(8,128)(2,1)S(1)}) %tuple.31, (s32[1024]{0:T(1024)S(1)}, s32[2,1024]{1,0:T(2,128)S(1)}, bf16[64,16384]{1,0:T(8,128)(2,1)S(1)}, s32[1024]{0:T(1024)S(1)}, ...), branch_computations={%region_0.2_spmd, %region_2.3_spmd} | conditional | flops 23344017408 | bytes 171008352
  12.0 5.2 %all-to-all-start.1 = ((bf16[8,400,128]{2,1,0:T(8,128)(2,1)}), bf16[8,400,128]{2,1,0:T(8,128)(2,1)S(1)}, u32[]{:S(2)}, u32[]{:S(2)}) async-start(bf16[8,400,128]{2,1,0:T(8,128)(2,1)} %get-tuple-element.46), calls=%async_computation.1 | async-start | bytes 1638400 | tf_op jit(solution)/shard_map/cond/branch_1_fun/all_to_all | solution.py:333
  17.1 7.0 %pack_amplitudes.1 = bf16[8,1280,128]{2,1,0:T(8,128)(2,1)S(1)} custom-call(s32[1024]{0:T(1024)S(1)} %get-tuple-element.40.irrep_s, s32[2,1024]{1,0:T(2,128)S(1)} %get-tuple-element.44.slots, bf16[64,16384]{1,0:T(8,128)(2,1)S(1)} %get-tuple-element.45.t_ref), custom_call_target="tpu_custom_call" | custom-call | flops 8000000000 | tf_op jit(solution)/shard_map/cond/branch_1_fun/pack_amplitudes/pallas_call | solution.py:335
  24.2 0.0 copy-start
  24.2 1.5 %copy-done = bf16[8,1280,128]{2,1,0:T(8,128)(2,1)} copy-done((bf16[8,1280,128]{2,1,0:T(8,128)(2,1)}, bf16[8,1280,128]{2,1,0:T(8,128)(2,1)S(1)}, u32[]{:S(2)}) %copy-start) | copy-done | bytes 2621464 | tf_op jit(solution)/shard_map/conditional.1
  25.7 3.5 %all-to-all-done.1.refs_0_ = bf16[8,400,128]{2,1,0:T(8,128)(2,1)S(1)} async-done(((bf16[8,400,128]{2,1,0:T(8,128)(2,1)}), bf16[8,400,128]{2,1,0:T(8,128)(2,1)S(1)}, u32[]{:S(2)}, u32[]{:S(2)}) %all-to-all-start.1) | async-done | bytes 819232 | tf_op jit(solution)/shard_map/cond/branch_1_fun/all_to_all | solution.py:333
  29.2 3.6 %all-to-all-start = ((bf16[8,1280,128]{2,1,0:T(8,128)(2,1)}), bf16[8,1280,128]{2,1,0:T(8,128)(2,1)S(1)}, u32[]{:S(2)}, u32[]{:S(2)}) async-start(bf16[8,1280,128]{2,1,0:T(8,128)(2,1)} %copy-done), calls=%async_computation | async-start | bytes 5242880 | tf_op jit(solution)/shard_map/cond/branch_1_fun/all_to_all | solution.py:348
  32.9 1.6 %collective-permute-start = (bf16[8,400,128]{2,1,0:T(8,128)(2,1)S(1)}, bf16[8,400,128]{2,1,0:T(8,128)(2,1)}, u32[]{:S(2)}, u32[]{:S(2)}) collective-permute-start(bf16[8,400,128]{2,1,0:T(8,128)(2,1)S(1)} %all-to-all-done.1.refs_0_), channel_id=1, source_target_pairs={{0,2},{2,4},{4,6},{6,0},{1,3},{3,5},{5,7},{7,1},{8,10},{10,12},{12... | collective-permute-start | bytes 2457608 | tf_op jit(solution)/shard_map/cond/branch_1_fun/ppermute | solution.py:318
  34.5 2.2 %collective-permute-start.2 = (bf16[8,400,128]{2,1,0:T(8,128)(2,1)S(1)}, bf16[8,400,128]{2,1,0:T(8,128)(2,1)}, u32[]{:S(2)}, u32[]{:S(2)}) collective-permute-start(bf16[8,400,128]{2,1,0:T(8,128)(2,1)S(1)} %all-to-all-done.1.refs_0_), channel_id=1, source_target_pairs={{0,6},{2,0},{4,2},{6,4},{1,7},{3,1},{5,3},{7,5},{8,14},{10,8},{12,... | collective-permute-start | bytes 2457608 | tf_op jit(solution)/shard_map/cond/branch_1_fun/ppermute | solution.py:320
  36.8 19.2 %collective-permute-done.refs_1_ = bf16[8,400,128]{2,1,0:T(8,128)(2,1)} collective-permute-done((bf16[8,400,128]{2,1,0:T(8,128)(2,1)S(1)}, bf16[8,400,128]{2,1,0:T(8,128)(2,1)}, u32[]{:S(2)}, u32[]{:S(2)}) %collective-permute-start) | collective-permute-done | bytes 819232 | tf_op jit(solution)/shard_map/cond/branch_1_fun/ppermute | solution.py:318
  55.9 0.0 collective-permute-start.1
  55.9 8.3 %all-to-all-done.t_ref = bf16[8,1280,128]{2,1,0:T(8,128)(2,1)S(1)} async-done(((bf16[8,1280,128]{2,1,0:T(8,128)(2,1)}), bf16[8,1280,128]{2,1,0:T(8,128)(2,1)S(1)}, u32[]{:S(2)}, u32[]{:S(2)}) %all-to-all-start) | async-done | bytes 2621472 | tf_op jit(solution)/shard_map/cond/branch_1_fun/all_to_all | solution.py:348
  64.2 4.9 %unpack_amplitudes.1.t_ref = bf16[3,1536,512]{2,1,0:T(8,128)(2,1)S(1)} custom-call(s32[1024]{0:T(1024)S(1)} %get-tuple-element.40.irrep_s, s32[1024]{0:T(1024)S(1)} %get-tuple-element.41.spin_s, s32[16,128]{1,0:T(8,128)S(1)} %get-tuple-element.43.offsets, s32[16,128]{1,0:T(8,128)S(1)} %get-tuple-element.42.counts, bf16[8,1280,128]{2,1,0:T(8,128)(2,1)S(1)} %all-to-all-done.t_ref), custom_call_target="tpu_custom_call" | custom-call | flops 6000000000 | tf_op jit(solution)/shard_map/cond/branch_1_fun/unpack_amplitudes/pallas_call | solution.py:349
  69.1 3.2 %collective-permute-done.2.refs_2_ = bf16[8,400,128]{2,1,0:T(8,128)(2,1)} collective-permute-done((bf16[8,400,128]{2,1,0:T(8,128)(2,1)S(1)}, bf16[8,400,128]{2,1,0:T(8,128)(2,1)}, u32[]{:S(2)}, u32[]{:S(2)}) %collective-permute-start.2) | collective-permute-done | bytes 819232 | tf_op jit(solution)/shard_map/cond/branch_1_fun/ppermute | solution.py:320
  72.4 7.3 %contract.2.refs_1_ = bf16[4,4,2,160,128]{4,3,2,1,0:T(8,128)(2,1)} custom-call(s32[1024]{0:T(1024)S(1)} %get-tuple-element.40.irrep_s, s32[1024]{0:T(1024)S(1)} %get-tuple-element.41.spin_s, s32[16,128]{1,0:T(8,128)S(1)} %get-tuple-element.42.counts, bf16[3,1536,512]{2,1,0:T(8,128)(2,1)S(1)} %unpack_amplitudes.1.t_ref, ...), custom_call_target="tpu_custom_call" | custom-call | flops 6000000000 | tf_op jit(solution)/shard_map/cond/branch_1_fun/contract/pallas_call | solution.py:374
  79.7 10.9 %collective-permute-done.1.refs_0_ = bf16[8,400,128]{2,1,0:T(8,128)(2,1)} collective-permute-done((bf16[8,400,128]{2,1,0:T(8,128)(2,1)}, bf16[8,400,128]{2,1,0:T(8,128)(2,1)}, u32[]{:S(2)}, u32[]{:S(2)}) %collective-permute-start.1) | collective-permute-done | bytes 819232 | tf_op jit(solution)/shard_map/cond/branch_1_fun/ppermute | solution.py:318
  90.6 3.6 %contract.3 = bf16[4,4,2,160,128]{4,3,2,1,0:T(8,128)(2,1)} custom-call(s32[1024]{0:T(1024)S(1)} %get-tuple-element.40.irrep_s, s32[1024]{0:T(1024)S(1)} %get-tuple-element.41.spin_s, s32[16,128]{1,0:T(8,128)S(1)} %get-tuple-element.42.counts, bf16[3,1536,512]{2,1,0:T(8,128)(2,1)S(1)} %unpack_amplitudes.1.t_ref, ...), custom_call_target="tpu_custom_call", output_to_operand_aliasing={{}: (5, {})} | custom-call | flops 2000000000 | tf_op jit(solution)/shard_map/cond/branch_1_fun/contract/pallas_call | solution.py:374
  94.2 4.1 %all-to-all-start.2 = ((bf16[32,160,128]{2,1,0:T(8,128)(2,1)}), bf16[32,160,128]{2,1,0:T(8,128)(2,1)S(1)}, u32[]{:S(2)}, u32[]{:S(2)}) async-start(bf16[32,160,128]{2,1,0:T(8,128)(2,1)} %bitcast.9), calls=%async_computation.2 | async-start | bytes 2621440 | tf_op jit(solution)/shard_map/cond/branch_1_fun/all_to_all | solution.py:386
  98.3 33.2 %all-to-all-done.2 = bf16[32,160,128]{2,1,0:T(8,128)(2,1)S(1)} async-done(((bf16[32,160,128]{2,1,0:T(8,128)(2,1)}), bf16[32,160,128]{2,1,0:T(8,128)(2,1)S(1)}, u32[]{:S(2)}, u32[]{:S(2)}) %all-to-all-start.2) | async-done | bytes 1310752 | tf_op jit(solution)/shard_map/cond/branch_1_fun/all_to_all | solution.py:386
  131.5 1.0 copy.24
  132.5 0.5 dot_general.10
  133.1 2.6 %bitcast_convert_fusion = bf16[512,1024]{1,0:T(8,128)(2,1)} fusion(bf16[512,4,2,160]{0,3,2,1:T(8,128)(2,1)S(1)} %dot_general.10, s32[1024]{0:T(1024)S(1)} %bitcast.47, s32[4,2,160]{2,1,0:T(2,128)S(1)} %multiply_add_fusion.1), kind=kOutput, calls=%fused_computation.15 | convolution fusion | flops 1344012288 | bytes 2368512 | tf_op jit(solution)/shard_map/cond/branch_1_fun/dot_general | solution.py:390
  (2 shorter events, 0.0 us)
Async XLA Ops:
  0.0 11.7 %copy-start.1 = (bf16[64,16384]{1,0:T(8,128)(2,1)S(1)}, bf16[64,16384]{1,0:T(8,128)(2,1)}, u32[]{:S(2)}) copy-start(bf16[64,16384]{1,0:T(8,128)(2,1)} %param.6) | copy-start | bytes 6291460
  0.0 11.7 %copy-start.2 = (s32[1024]{0:T(1024)S(1)}, s32[1024]{0:T(1024)}, u32[]{:S(2)}) copy-start(s32[1024]{0:T(1024)} %irrep_s.1) | copy-start | bytes 12292
  0.0 11.7 %copy-start.3 = (s32[1024]{0:T(1024)S(1)}, s32[1024]{0:T(1024)}, u32[]{:S(2)}) copy-start(s32[1024]{0:T(1024)} %spin_s.1) | copy-start | bytes 12292
  12.0 17.3 %all-to-all-start.1 = ((bf16[8,400,128]{2,1,0:T(8,128)(2,1)}), bf16[8,400,128]{2,1,0:T(8,128)(2,1)S(1)}, u32[]{:S(2)}, u32[]{:S(2)}) async-start(bf16[8,400,128]{2,1,0:T(8,128)(2,1)} %get-tuple-element.46), calls=%async_computation.1 | async-start | bytes 1638400 | tf_op jit(solution)/shard_map/cond/branch_1_fun/all_to_all | solution.py:333
  24.2 1.5 %copy-start = (bf16[8,1280,128]{2,1,0:T(8,128)(2,1)}, bf16[8,1280,128]{2,1,0:T(8,128)(2,1)S(1)}, u32[]{:S(2)}) copy-start(bf16[8,1280,128]{2,1,0:T(8,128)(2,1)S(1)} %pack_amplitudes.1) | copy-start | bytes 7864324 | tf_op jit(solution)/shard_map/conditional.1
  29.2 35.0 %all-to-all-start = ((bf16[8,1280,128]{2,1,0:T(8,128)(2,1)}), bf16[8,1280,128]{2,1,0:T(8,128)(2,1)S(1)}, u32[]{:S(2)}, u32[]{:S(2)}) async-start(bf16[8,1280,128]{2,1,0:T(8,128)(2,1)} %copy-done), calls=%async_computation | async-start | bytes 5242880 | tf_op jit(solution)/shard_map/cond/branch_1_fun/all_to_all | solution.py:348
  32.9 23.1 %collective-permute-start = (bf16[8,400,128]{2,1,0:T(8,128)(2,1)S(1)}, bf16[8,400,128]{2,1,0:T(8,128)(2,1)}, u32[]{:S(2)}, u32[]{:S(2)}) collective-permute-start(bf16[8,400,128]{2,1,0:T(8,128)(2,1)S(1)} %all-to-all-done.1.refs_0_), channel_id=1, source_target_pairs={{0,2},{2,4},{4,6},{6,0},{1,3},{3,5},{5,7},{7,1},{8,10},{10,12},{12... | collective-permute-start | bytes 2457608 | tf_op jit(solution)/shard_map/cond/branch_1_fun/ppermute | solution.py:318
  34.5 37.9 %collective-permute-start.2 = (bf16[8,400,128]{2,1,0:T(8,128)(2,1)S(1)}, bf16[8,400,128]{2,1,0:T(8,128)(2,1)}, u32[]{:S(2)}, u32[]{:S(2)}) collective-permute-start(bf16[8,400,128]{2,1,0:T(8,128)(2,1)S(1)} %all-to-all-done.1.refs_0_), channel_id=1, source_target_pairs={{0,6},{2,0},{4,2},{6,4},{1,7},{3,1},{5,3},{7,5},{8,14},{10,8},{12,... | collective-permute-start | bytes 2457608 | tf_op jit(solution)/shard_map/cond/branch_1_fun/ppermute | solution.py:320
  55.9 34.6 %collective-permute-start.1 = (bf16[8,400,128]{2,1,0:T(8,128)(2,1)}, bf16[8,400,128]{2,1,0:T(8,128)(2,1)}, u32[]{:S(2)}, u32[]{:S(2)}) collective-permute-start(bf16[8,400,128]{2,1,0:T(8,128)(2,1)} %collective-permute-done.refs_1_), channel_id=1, source_target_pairs={{0,2},{2,4},{4,6},{6,0},{1,3},{3,5},{5,7},{7,1},{8,10},{10,12},{12... | collective-permute-start | bytes 2457608 | tf_op jit(solution)/shard_map/cond/branch_1_fun/ppermute | solution.py:318
  94.2 37.3 %all-to-all-start.2 = ((bf16[32,160,128]{2,1,0:T(8,128)(2,1)}), bf16[32,160,128]{2,1,0:T(8,128)(2,1)S(1)}, u32[]{:S(2)}, u32[]{:S(2)}) async-start(bf16[32,160,128]{2,1,0:T(8,128)(2,1)} %bitcast.9), calls=%async_computation.2 | async-start | bytes 2621440 | tf_op jit(solution)/shard_map/cond/branch_1_fun/all_to_all | solution.py:386

commit v3 on v2

--- a/solution.py
+++ b/solution.py
@@ -52,7 +52,7 @@
 def pack_integrals_kernel(
     c_count, c_total, subs, cap, label_cap, irrep_s, spin_s, irrep_v, spin_v, v_hbm, *refs
 ):
-    out, slots_out, offsets_out, counts_out, fits_out, v_ref, arrived = refs
+    out, slots_out, offsets_out, counts_out, fits_out, v_ref, arrived, ends_ref, tail_ref = refs
     virtuals = v_ref.shape[1]
     copies = []
     for i in range(c_count):
@@ -113,10 +113,17 @@
     offsets = jnp.zeros((c_total, LANES), jnp.int32)
     for k in range(1, c_count):
         offsets += jnp.where(within >= k, pltpu.roll(sizes, k, 0), 0)
-    offsets_out[...] = offsets
+    ends = offsets + sizes
+    offsets_out[:c_total, :] = offsets
+    ends_ref[...] = ends
+    over = jnp.zeros((1, LANES), jnp.int32)
+    for r in range(c_total // c_count):
+        offsets_out[c_total + r : c_total + r + 1, :] = over
+        last = (r + 1) * c_count - 1
+        over = over + jnp.maximum(ends[last : last + 1, :] - 256, 0)
     irrep_most = jnp.max(counts[:IRREPS] + counts[IRREPS:])
-    label_most = jnp.max(offsets + sizes)
-    fits_out[0] = jnp.where((irrep_most <= cap) & (label_most <= label_cap), 1, 0)
+    fit = (irrep_most <= cap) & (jnp.max(ends) <= label_cap) & (jnp.max(over) <= LANES)
+    fits_out[0] = jnp.where(fit, 1, 0)
 
     row_label = jnp.bitwise_xor(irrep, irrep_s[a]) + 8 * (spin + spin_s[a])
     row_slot = jnp.bitwise_xor(irrep, irrep_s[a]) * cap + rank8
@@ -141,18 +148,31 @@
     columns = lines.astype(jnp.float32).T.astype(jnp.int32)
     row_label = columns[:, c_count : c_count + 1]
 
-    front = None
+    tail_ref[...] = jnp.zeros_like(tail_ref)
+    lane = lax.broadcasted_iota(jnp.int32, (virtuals, 256), 1)
+    tail_lane = 256 + lax.broadcasted_iota(jnp.int32, (virtuals, LANES), 1) % 64
+    main = None
     for i in range(c_count):
+        longest = jnp.max(ends_ref[pl.ds(row * c_count + i, 1), :])
         copies[i].wait()
         masked = jnp.where(
             row_label == cd_label[i : i + 1], v_ref[i], jnp.zeros((), v_ref.dtype)
         )
-        lane = lax.broadcasted_iota(jnp.int32, (virtuals, 384), 1)
-        lane = jnp.where(lane >= 320, lane - 64, lane)
-        place = (columns[:, i : i + 1] == lane).astype(jnp.bfloat16)
-        term = jnp.dot(masked, place, preferred_element_type=jnp.float32)
-        front = term if front is None else front + term
-    front = front.astype(jnp.bfloat16)
+        slot = columns[:, i : i + 1]
+        term = jnp.dot(
+            masked, (slot == lane).astype(jnp.bfloat16), preferred_element_type=jnp.float32
+        )
+        main = term if main is None else main + term
+
+        @pl.when(longest > 256)
+        def _(masked=masked, slot=slot):
+            tail_ref[...] += jnp.dot(
+                masked,
+                (slot == tail_lane).astype(jnp.bfloat16),
+                preferred_element_type=jnp.float32,
+            )
+
+    front = jnp.concatenate([main, tail_ref[...]], axis=1).astype(jnp.bfloat16)
     for g in range(IRREPS):
         spot = lax.broadcasted_iota(jnp.int32, (cap, virtuals), 0) + g * cap
         rows = (row_slot == spot).astype(jnp.bfloat16)
@@ -193,7 +213,7 @@
 
 
 def unpack_amplitudes_kernel(
-    rows, subs, c_total, cap, pairs, irrep_s, spin_s, offsets, counts, t_ref, out_ref, quarter
+    rows, subs, c_total, cap, pairs, irrep_s, spin_s, offsets, counts, t_ref, out_ref, quarter, tails
 ):
     mine = lax.axis_index("row") * subs + lax.axis_index("sub")
     fold = LANES // pairs
@@ -203,8 +223,7 @@
     group = out_ref.shape[2]
     main = rows * 256
     share = lax.broadcasted_iota(jnp.int32, (cap, LANES), 1) // pairs
-    spot = lax.broadcasted_iota(jnp.int32, (384, wide), 0)
-    spot = jnp.where(spot >= 320, spot - 64, spot)
+    spot = lax.broadcasted_iota(jnp.int32, (256 + LANES, wide), 0)
     lane = lax.broadcasted_iota(jnp.int32, (1, wide), 1)
     for r in range(rows):
         for i in range(c_count):
@@ -232,13 +251,52 @@
                 inside = (place >= least) & (place < most) & (place >= 0) & (place < cap)
                 start = offsets[c, mine + 8 * s]
                 target = jnp.where(inside, place + (start - least), target)
+            over = offsets[c_total + r, mine + 8 * s]
+            target = jnp.where(target >= 256, target + over, target)
             part = jnp.dot(
                 (target == spot).astype(jnp.bfloat16),
                 quarter[...],
                 preferred_element_type=jnp.float32,
-            ).astype(jnp.bfloat16)
-            out_ref[s, r * 256 : (r + 1) * 256, :] = part[:256]
-            out_ref[s, main + r * 128 : main + (r + 1) * 128, :] = part[256:]
+            )
+            out_ref[s, r * 256 : (r + 1) * 256, :] = part[:256].astype(jnp.bfloat16)
+            tails[s] = part[256:] if r == 0 else tails[s] + part[256:]
+    for s in range(3):
+        out_ref[s, main:, :] = tails[s].astype(jnp.bfloat16)
+
+
+def join_kernel(rows, subs, cap, irrep_s, spin_s, offsets, counts, v_ref, out_ref):
+    plane = lax.axis_index("plane")
+    mine = lax.axis_index("row") * subs + lax.axis_index("sub")
+    c_total = offsets.shape[0] - rows
+    half = cap // 2
+    main = 2 * cap
+    for source in range(rows * subs):
+        out_ref[source * main : (source + 1) * main, :] = v_ref[source, :main, :]
+    left = lax.broadcasted_iota(jnp.int32, (half, LANES), 1) < 64
+    place = lax.broadcasted_iota(jnp.int32, (LANES, LANES), 0) % 64
+    lane = lax.broadcasted_iota(jnp.int32, (LANES, LANES), 1)
+    slot = lax.broadcasted_iota(jnp.int32, (cap, LANES), 0)
+    for y in range(subs):
+        a = plane * subs + y
+        low = counts[jnp.bitwise_xor(irrep_s[a], mine), 0]
+        joined = [jnp.zeros((cap, LANES), jnp.float32) for _ in range(2)]
+        for r in range(rows):
+            tail = v_ref[r * subs + y, main:, :]
+            none = jnp.zeros((), tail.dtype)
+            wide = jnp.concatenate(
+                [jnp.where(left, tail, none), jnp.where(left, none, tail)], axis=0
+            )
+            for k in range(2):
+                over = offsets[c_total + r, mine + 8 * (spin_s[a] + k)]
+                joined[k] += jnp.dot(
+                    wide,
+                    (place + over == lane).astype(jnp.bfloat16),
+                    preferred_element_type=jnp.float32,
+                )
+        at = rows * subs * main + y * cap
+        out_ref[at : at + cap, :] = jnp.where(slot < low, joined[0], joined[1]).astype(
+            jnp.bfloat16
+        )
 
 
 def shift_of(k):
@@ -254,23 +312,18 @@
     plane = lax.axis_index("plane")
     mine = lax.axis_index("row") * subs + lax.axis_index("sub")
     n, pairs = out_ref.shape[3:]
-    half = n // 2
     main = rows * 256
-    left = lax.broadcasted_iota(jnp.int32, (half, LANES), 1) < 64
     for k, v_ref in enumerate(v_refs):
         for y in range(subs):
             top = y * n
             for r in range(rows):
-                source = r * subs + y
-                at = main + r * 128
-                v_rows[k, top : top + n, r * 256 : r * 256 + 128] = v_ref[source, :n, :]
+                at = (r * subs + y) * 2 * n
+                v_rows[k, top : top + n, r * 256 : r * 256 + 128] = v_ref[at : at + n, :]
                 v_rows[k, top : top + n, r * 256 + 128 : (r + 1) * 256] = v_ref[
-                    source, n : 2 * n, :
+                    at + n : at + 2 * n, :
                 ]
-                tail = v_ref[source, 2 * n :, :]
-                none = jnp.zeros((), tail.dtype)
-                v_rows[k, top : top + half, at : at + 128] = jnp.where(left, tail, none)
-                v_rows[k, top + half : top + n, at : at + 128] = jnp.where(left, none, tail)
+            at = rows * subs * 2 * n + y * n
+            v_rows[k, top : top + n, main:] = v_ref[at : at + n, :]
     slot = lax.broadcasted_iota(jnp.int32, (n, rows * pairs), 0)
 
     def one_plane(k, carry):
@@ -331,6 +384,15 @@
     plane_axes, all_axes = ("row", "sub"), ("row", "plane", "sub")
 
     v_plane = lax.all_to_all(v_packed, plane_axes, 0, 0, tiled=True)
+    v_plane = pl.pallas_call(
+        functools.partial(join_kernel, rows, subs, cap),
+        out_shape=jax.ShapeDtypeStruct((subs * cap * (2 * rows + 1), LANES), jnp.bfloat16),
+        in_specs=[SMEM] * 4 + [VMEM],
+        out_specs=VMEM,
+        compiler_params=options(),
+        cost_estimate=cost(1.5),
+        name="join_tails",
+    )(irrep, spin, offsets, counts, v_plane)
     found = ring_gather(v_plane, planes)
     t_packed = pl.pallas_call(
         functools.partial(pack_amplitudes_kernel, c_total, cap),
@@ -348,10 +410,13 @@
     t_mine = lax.all_to_all(t_packed, plane_axes, 0, 0, tiled=True)
     t_labels = pl.pallas_call(
         functools.partial(unpack_amplitudes_kernel, rows, subs, c_total, cap, pairs),
-        out_shape=jax.ShapeDtypeStruct((3, rows * 384, group), jnp.bfloat16),
+        out_shape=jax.ShapeDtypeStruct((3, rows * 256 + LANES, group), jnp.bfloat16),
         in_specs=[SMEM] * 4 + [VMEM],
         out_specs=VMEM,
-        scratch_shapes=[pltpu.VMEM((c_total // rows * cap, group), jnp.bfloat16)],
+        scratch_shapes=[
+            pltpu.VMEM((c_total // rows * cap, group), jnp.bfloat16),
+            pltpu.VMEM((3, LANES, group), jnp.float32),
+        ],
         compiler_params=options(),
         cost_estimate=cost(6),
         name="unpack_amplitudes",
@@ -362,7 +427,7 @@
     for first, last in ((0, planes - 1), (planes - 1, planes)):
         shape = (rows, planes, subs, cap, group // rows)
         scratch = [
-            pltpu.VMEM((last - first, subs * cap, rows * 384), jnp.bfloat16),
+            pltpu.VMEM((last - first, subs * cap, rows * 256 + LANES), jnp.bfloat16),
             pltpu.VMEM((3, subs * cap, group), jnp.float32),
         ]
         if first:
@@ -384,6 +449,12 @@
         )(irrep, spin, counts, t_labels, *blocks, *([result] if first else []))
     result = result.reshape(rows * planes * subs, cap, group // rows)
     back = lax.all_to_all(result, all_axes, 0, 0, tiled=True)
+    return back
+
+
+def put_back(rows, planes, subs, back, slots):
+    cap, group = back.shape[1], back.shape[2] * rows
+    virtuals = slots.shape[1]
     back = back.reshape(rows, planes, subs, cap, group // rows)
     spots = jnp.arange(IRREPS * cap, dtype=jnp.int32)
     rows_back = (spots[:, None] == slots[0]).astype(jnp.bfloat16)
@@ -409,7 +480,7 @@
         out_shape=[
             jax.ShapeDtypeStruct((IRREPS, cap * 5 // 2, LANES), jnp.bfloat16),
             jax.ShapeDtypeStruct((2, virtuals), jnp.int32),
-            jax.ShapeDtypeStruct((c_total, LANES), jnp.int32),
+            jax.ShapeDtypeStruct((c_total + rows, LANES), jnp.int32),
             jax.ShapeDtypeStruct((2 * IRREPS, LANES), jnp.int32),
             jax.ShapeDtypeStruct((1,), jnp.int32),
         ],
@@ -418,16 +489,17 @@
         scratch_shapes=[
             pltpu.VMEM((c_count, virtuals, virtuals), jnp.bfloat16),
             pltpu.SemaphoreType.DMA((c_count,)),
+            pltpu.VMEM((c_total, LANES), jnp.int32),
+            pltpu.VMEM((virtuals, LANES), jnp.float32),
         ],
         compiler_params=options(),
         cost_estimate=cost(9),
         name="pack_integrals",
     )(irrep, spin, irrep[None, :], spin[None, :], integrals)
+    back = packed(rows, planes, subs, amplitudes, irrep, spin, v_packed, slots, offsets, counts)
     return lax.cond(
         fits[0] > 0,
-        lambda: packed(
-            rows, planes, subs, amplitudes, irrep, spin, v_packed, slots, offsets, counts
-        ),
+        lambda: put_back(rows, planes, subs, back, slots),
         lambda: dense(rows, planes * subs, amplitudes, integrals, irrep, spin),
     )
 

time: 136 us -> 130 us (0.956)
  waiting for transfers between devices: 78.3 us -> 72.3 us
  Pallas kernels: 33.9 us -> 35.7 us
    ppermute x2, waiting for transfers between devices: 30 us -> 27.4 us  [ring_gather(): found[-step] = lax.ppermute(found[1 - step], 'plane', up)]
    unnamed x6 -> x10, local copies, waits for them, and re-layouts: 0.01 us -> 2.47 us
    pallas_call x0 -> x1, Pallas kernels: none -> 2.21 us  [packed(): pl.pallas_call(functools.partial(join_kernel, rows, subs, cap), out_shape...]
    another operation x2 -> x0, local copies, waits for them, and re-layouts: 1.49 us -> none
  transfers between devices with their start and end apart: 6 -> 6, of which waited for: 6 -> 6; matrix products, arithmetic and copies ran while one was open for 0% -> 0% of each run, Pallas kernels for 14% -> 17%
where the time goes in v3:
time: 130 us
  waiting for transfers between devices  72.3 us (56%)
  Pallas kernels  35.7 us (27%)
  starting transfers between devices  16.7 us (13%)
  local copies, waits for them, and re-layouts  2.47 us (2%)
  matrix products  1.74 us (1%)
    all_to_all x1, waiting for transfers between devices, packed(): back = lax.all_to_all(result, all_axes, 0, 0, tiled=True)  32.6 us
    ppermute x2, waiting for transfers between devices, ring_gather(): found[-step] = lax.ppermute(found[1 - step], 'plane', up)  27.4 us
    pallas_call x1, Pallas kernels, local(): pl.pallas_call(functools.partial(pack_integrals_kernel, c_count, c_total,...  10.5 us
    pallas_call x2, Pallas kernels, packed(): pl.pallas_call(functools.partial(contract_kernel, rows, planes, subs, fir...  9.89 us
    pallas_call x1, Pallas kernels, packed(): pl.pallas_call(functools.partial(pack_amplitudes_kernel, c_total, cap), o...  8.07 us
    all_to_all x1, waiting for transfers between devices, packed(): t_mine = lax.all_to_all(t_packed, plane_axes, 0, 0, tiled=True)  7.75 us
    all_to_all x1, starting transfers between devices, packed(): v_plane = lax.all_to_all(v_packed, plane_axes, 0, 0, tiled=True)  5.19 us
    pallas_call x1, Pallas kernels, packed(): pl.pallas_call(functools.partial(unpack_amplitudes_kernel, rows, subs, c_...  5.05 us
  transfers between devices with their start and end apart: 6, of which 6 were waited for; matrix products, arithmetic and copies ran while one was open for 0% of the time, Pallas kernels for 17%

profile of v3, /device:TPU:0, one launch (start us, length us, event | category | flops | bytes accessed | tf_op | source)
XLA Modules:
  0.0 129.6 jit_solution(14463837626014116128)
XLA Ops:
  0.0 0.0 copy-start.3
  0.0 10.5 %pack_integrals.1 = (bf16[8,400,128]{2,1,0:T(8,128)(2,1)}, s32[2,1024]{1,0:T(2,128)S(1)}, s32[20,128]{1,0:T(8,128)S(1)}, s32[16,128]{1,0:T(8,128)S(1)}, s32[1]{0:T(128)}) custom-call(s32[1024]{0:T(1024)} %irrep_s.11, s32[1024]{0:T(1024)} %spin_s.9, s32[1,1024]{1,0:T(1,128)} %bitcast.50, s32[1,1024]{1,0:T(1,128)} %bitcast.51, bf16[1024,4096]{1,0:T(8,128)(2,1)} %v_hbm.1), custom_call_target="tpu_custom_call" | custom-call | flops 8999999488 | tf_op jit(solution)/shard_map/pack_integrals/pallas_call | solution.py:476
  10.5 5.2 %all-to-all-start.4 = ((bf16[8,400,128]{2,1,0:T(8,128)(2,1)}), bf16[8,400,128]{2,1,0:T(8,128)(2,1)S(1)}, u32[]{:S(2)}, u32[]{:S(2)}) async-start(bf16[8,400,128]{2,1,0:T(8,128)(2,1)} %get-tuple-element.41), calls=%async_computation.4 | async-start | bytes 1638400 | tf_op jit(solution)/shard_map/all_to_all | solution.py:386
  15.7 0.0 copy-done.3
  15.7 0.0 copy-start.4
  15.7 8.1 %pack_amplitudes.1 = bf16[8,1280,128]{2,1,0:T(8,128)(2,1)S(1)} custom-call(s32[1024]{0:T(1024)S(1)} %copy-done.3, s32[2,1024]{1,0:T(2,128)S(1)} %get-tuple-element.38.slots, bf16[64,16384]{1,0:T(8,128)(2,1)} %t_ref.1), custom_call_target="tpu_custom_call" | custom-call | flops 8000000000 | tf_op jit(solution)/shard_map/pack_amplitudes/pallas_call | solution.py:397
  23.8 0.0 copy-start
  23.8 1.5 %copy-done = bf16[8,1280,128]{2,1,0:T(8,128)(2,1)} copy-done((bf16[8,1280,128]{2,1,0:T(8,128)(2,1)}, bf16[8,1280,128]{2,1,0:T(8,128)(2,1)S(1)}, u32[]{:S(2)}) %copy-start) | copy-done | bytes 2621464
  25.3 2.5 %all-to-all-done.4.v_ref = bf16[8,400,128]{2,1,0:T(8,128)(2,1)S(1)} async-done(((bf16[8,400,128]{2,1,0:T(8,128)(2,1)}), bf16[8,400,128]{2,1,0:T(8,128)(2,1)S(1)}, u32[]{:S(2)}, u32[]{:S(2)}) %all-to-all-start.4) | async-done | bytes 819232 | tf_op jit(solution)/shard_map/all_to_all | solution.py:386
  27.8 3.6 %all-to-all-start.3 = ((bf16[8,1280,128]{2,1,0:T(8,128)(2,1)}), bf16[8,1280,128]{2,1,0:T(8,128)(2,1)S(1)}, u32[]{:S(2)}, u32[]{:S(2)}) async-start(bf16[8,1280,128]{2,1,0:T(8,128)(2,1)} %copy-done), calls=%async_computation.3 | async-start | bytes 5242880 | tf_op jit(solution)/shard_map/all_to_all | solution.py:410
  31.4 0.0 copy-done.4
  31.4 2.2 %join_tails.1.refs_0_ = bf16[2880,128]{1,0:T(8,128)(2,1)} custom-call(s32[1024]{0:T(1024)S(1)} %copy-done.3, s32[1024]{0:T(1024)S(1)} %copy-done.4, s32[20,128]{1,0:T(8,128)S(1)} %get-tuple-element.40.offsets, s32[16,128]{1,0:T(8,128)S(1)} %get-tuple-element.39.counts, bf16[8,400,128]{2,1,0:T(8,128)(2,1)S(1)} %all-to-all-done.4.v_ref), custom_call_target="tpu_custom_call" | custom-call | flops 1500000000 | tf_op jit(solution)/shard_map/join_tails/pallas_call | solution.py:387
  33.6 1.6 %collective-permute-start = (bf16[2880,128]{1,0:T(8,128)(2,1)}, bf16[2880,128]{1,0:T(8,128)(2,1)S(1)}, u32[]{:S(2)}, u32[]{:S(2)}) collective-permute-start(bf16[2880,128]{1,0:T(8,128)(2,1)} %join_tails.1.refs_0_), channel_id=1, source_target_pairs={{0,2},{2,4},{4,6},{6,0},{1,3},{3,5},{5,7},{7,1},{8,10},{10,12},{12... | collective-permute-start | bytes 2211848 | tf_op jit(solution)/shard_map/ppermute | solution.py:371
  35.2 2.2 %collective-permute-start.2 = (bf16[2880,128]{1,0:T(8,128)(2,1)}, bf16[2880,128]{1,0:T(8,128)(2,1)}, u32[]{:S(2)}, u32[]{:S(2)}) collective-permute-start(bf16[2880,128]{1,0:T(8,128)(2,1)} %join_tails.1.refs_0_), channel_id=1, source_target_pairs={{0,6},{2,0},{4,2},{6,4},{1,7},{3,1},{5,3},{7,5},{8,14},{10,8},{12,... | collective-permute-start | bytes 2211848 | tf_op jit(solution)/shard_map/ppermute | solution.py:373
  37.4 17.5 %collective-permute-done.refs_1_ = bf16[2880,128]{1,0:T(8,128)(2,1)S(1)} collective-permute-done((bf16[2880,128]{1,0:T(8,128)(2,1)}, bf16[2880,128]{1,0:T(8,128)(2,1)S(1)}, u32[]{:S(2)}, u32[]{:S(2)}) %collective-permute-start) | collective-permute-done | bytes 737312 | tf_op jit(solution)/shard_map/ppermute | solution.py:371
  55.0 0.0 collective-permute-start.1
  55.0 7.8 %all-to-all-done.3.t_ref = bf16[8,1280,128]{2,1,0:T(8,128)(2,1)S(1)} async-done(((bf16[8,1280,128]{2,1,0:T(8,128)(2,1)}), bf16[8,1280,128]{2,1,0:T(8,128)(2,1)S(1)}, u32[]{:S(2)}, u32[]{:S(2)}) %all-to-all-start.3) | async-done | bytes 2621472 | tf_op jit(solution)/shard_map/all_to_all | solution.py:410
  62.7 5.0 %unpack_amplitudes.1.t_ref = bf16[3,1152,512]{2,1,0:T(8,128)(2,1)S(1)} custom-call(s32[1024]{0:T(1024)S(1)} %copy-done.3, s32[1024]{0:T(1024)S(1)} %copy-done.4, s32[20,128]{1,0:T(8,128)S(1)} %get-tuple-element.40.offsets, s32[16,128]{1,0:T(8,128)S(1)} %get-tuple-element.39.counts, bf16[8,1280,128]{2,1,0:T(8,128)(2,1)S(1)} %all-to-all-done.3.t_ref), custom_call_target="tpu_custom_call" | custom-call | flops 6000000000 | tf_op jit(solution)/shard_map/unpack_amplitudes/pallas_call | solution.py:411
  67.8 2.1 %collective-permute-done.2.refs_2_ = bf16[2880,128]{1,0:T(8,128)(2,1)} collective-permute-done((bf16[2880,128]{1,0:T(8,128)(2,1)}, bf16[2880,128]{1,0:T(8,128)(2,1)}, u32[]{:S(2)}, u32[]{:S(2)}) %collective-permute-start.2) | collective-permute-done | bytes 737312 | tf_op jit(solution)/shard_map/ppermute | solution.py:373
  69.9 6.5 %contract.2.refs_1_ = bf16[4,4,2,160,128]{4,3,2,1,0:T(8,128)(2,1)} custom-call(s32[1024]{0:T(1024)S(1)} %copy-done.3, s32[1024]{0:T(1024)S(1)} %copy-done.4, s32[16,128]{1,0:T(8,128)S(1)} %get-tuple-element.39.counts, bf16[3,1152,512]{2,1,0:T(8,128)(2,1)S(1)} %unpack_amplitudes.1.t_ref, bf16[2880,128]{1,0:T(8,128)(2,1)} %join_tails.1.refs_0_, ...), custom_call_target="tpu_custom_call" | custom-call | flops 6000000000 | tf_op jit(solution)/shard_map/contract/pallas_call | solution.py:439
  76.4 0.0 copy-start.1
  76.4 9.8 %collective-permute-done.1.refs_0_ = bf16[2880,128]{1,0:T(8,128)(2,1)} collective-permute-done((bf16[2880,128]{1,0:T(8,128)(2,1)S(1)}, bf16[2880,128]{1,0:T(8,128)(2,1)}, u32[]{:S(2)}, u32[]{:S(2)}) %collective-permute-start.1) | collective-permute-done | bytes 737312 | tf_op jit(solution)/shard_map/ppermute | solution.py:371
  86.2 3.4 %contract.3 = bf16[4,4,2,160,128]{4,3,2,1,0:T(8,128)(2,1)} custom-call(s32[1024]{0:T(1024)S(1)} %copy-done.3, s32[1024]{0:T(1024)S(1)} %copy-done.4, s32[16,128]{1,0:T(8,128)S(1)} %get-tuple-element.39.counts, bf16[3,1152,512]{2,1,0:T(8,128)(2,1)S(1)} %unpack_amplitudes.1.t_ref, ...), custom_call_target="tpu_custom_call", output_to_operand_aliasing={{}: (5, {})} | custom-call | flops 2000000000 | tf_op jit(solution)/shard_map/contract/pallas_call | solution.py:439
  89.6 4.1 %all-to-all-start.5 = ((bf16[32,160,128]{2,1,0:T(8,128)(2,1)}), bf16[32,160,128]{2,1,0:T(8,128)(2,1)S(1)}, u32[]{:S(2)}, u32[]{:S(2)}) async-start(bf16[32,160,128]{2,1,0:T(8,128)(2,1)} %bitcast.20), calls=%async_computation.5 | async-start | bytes 2621440 | tf_op jit(solution)/shard_map/all_to_all | solution.py:451
  94.3 32.6 %all-to-all-done.5 = bf16[32,160,128]{2,1,0:T(8,128)(2,1)S(1)} async-done(((bf16[32,160,128]{2,1,0:T(8,128)(2,1)}), bf16[32,160,128]{2,1,0:T(8,128)(2,1)S(1)}, u32[]{:S(2)}, u32[]{:S(2)}) %all-to-all-start.5) | async-done | bytes 1310752 | tf_op jit(solution)/shard_map/all_to_all | solution.py:451
  126.9 0.0 copy-done.1
  126.9 1.8 %conditional.6 = (bf16[512,1024]{1,0:T(8,128)(2,1)S(1)}) conditional(s32[]{:T(128)} %bitcast.19, (s32[1024]{0:T(1024)S(1)}, s32[1024]{0:T(1024)S(1)}, bf16[1024,4096]{1,0:T(8,128)(2,1)}, bf16[64,16384]{1,0:T(8,128)(2,1)S(1)}) %tuple.30, (s32[2,1024]{1,0:T(2,128)S(1)}, bf16[32,160,128]{2,1,0:T(8,128)(2,1)S(1)}) %tuple.22), branch_computations={%region_0.2_spmd, %region_2.3_spmd} | conditional | flops 17189851136 | bytes 171008352
  126.9 1.7 %bitcast_convert_fusion = bf16[1024,4,128]{0,2,1:T(8,128)(2,1)S(1)} fusion(bf16[4,4,2,160,128]{4,3,2,1,0:T(8,128)(2,1)S(1)} %bitcast.47, s32[1024]{0:T(1024)S(1)} %bitcast.53, s32[4,2,160]{2,1,0:T(2,128)S(1)} %multiply_add_fusion.1), kind=kOutput, calls=%fused_computation.16 | convolution fusion | flops 1344012288 | bytes 2368512 | tf_op jit(solution)/shard_map/cond/branch_1_fun/dot_general | solution.py:461
  128.7 0.0 copy-start.2
  128.7 1.0 copy-done.2
  (2 shorter events, 0.0 us)
Async XLA Ops:
  0.0 15.7 %copy-start.3 = (s32[1024]{0:T(1024)S(1)}, s32[1024]{0:T(1024)}, u32[]{:S(2)}) copy-start(s32[1024]{0:T(1024)} %irrep_s.11) | copy-start | bytes 12292
  10.5 17.3 %all-to-all-start.4 = ((bf16[8,400,128]{2,1,0:T(8,128)(2,1)}), bf16[8,400,128]{2,1,0:T(8,128)(2,1)S(1)}, u32[]{:S(2)}, u32[]{:S(2)}) async-start(bf16[8,400,128]{2,1,0:T(8,128)(2,1)} %get-tuple-element.41), calls=%async_computation.4 | async-start | bytes 1638400 | tf_op jit(solution)/shard_map/all_to_all | solution.py:386
  15.7 15.7 %copy-start.4 = (s32[1024]{0:T(1024)S(1)}, s32[1024]{0:T(1024)}, u32[]{:S(2)}) copy-start(s32[1024]{0:T(1024)} %spin_s.9) | copy-start | bytes 12292
  23.8 1.5 %copy-start = (bf16[8,1280,128]{2,1,0:T(8,128)(2,1)}, bf16[8,1280,128]{2,1,0:T(8,128)(2,1)S(1)}, u32[]{:S(2)}) copy-start(bf16[8,1280,128]{2,1,0:T(8,128)(2,1)S(1)} %pack_amplitudes.1) | copy-start | bytes 7864324
  27.8 35.0 %all-to-all-start.3 = ((bf16[8,1280,128]{2,1,0:T(8,128)(2,1)}), bf16[8,1280,128]{2,1,0:T(8,128)(2,1)S(1)}, u32[]{:S(2)}, u32[]{:S(2)}) async-start(bf16[8,1280,128]{2,1,0:T(8,128)(2,1)} %copy-done), calls=%async_computation.3 | async-start | bytes 5242880 | tf_op jit(solution)/shard_map/all_to_all | solution.py:410
  33.6 21.3 %collective-permute-start = (bf16[2880,128]{1,0:T(8,128)(2,1)}, bf16[2880,128]{1,0:T(8,128)(2,1)S(1)}, u32[]{:S(2)}, u32[]{:S(2)}) collective-permute-start(bf16[2880,128]{1,0:T(8,128)(2,1)} %join_tails.1.refs_0_), channel_id=1, source_target_pairs={{0,2},{2,4},{4,6},{6,0},{1,3},{3,5},{5,7},{7,1},{8,10},{10,12},{12... | collective-permute-start | bytes 2211848 | tf_op jit(solution)/shard_map/ppermute | solution.py:371
  35.2 34.7 %collective-permute-start.2 = (bf16[2880,128]{1,0:T(8,128)(2,1)}, bf16[2880,128]{1,0:T(8,128)(2,1)}, u32[]{:S(2)}, u32[]{:S(2)}) collective-permute-start(bf16[2880,128]{1,0:T(8,128)(2,1)} %join_tails.1.refs_0_), channel_id=1, source_target_pairs={{0,6},{2,0},{4,2},{6,4},{1,7},{3,1},{5,3},{7,5},{8,14},{10,8},{12,... | collective-permute-start | bytes 2211848 | tf_op jit(solution)/shard_map/ppermute | solution.py:373
  55.0 31.3 %collective-permute-start.1 = (bf16[2880,128]{1,0:T(8,128)(2,1)S(1)}, bf16[2880,128]{1,0:T(8,128)(2,1)}, u32[]{:S(2)}, u32[]{:S(2)}) collective-permute-start(bf16[2880,128]{1,0:T(8,128)(2,1)S(1)} %collective-permute-done.refs_1_), channel_id=1, source_target_pairs={{0,2},{2,4},{4,6},{6,0},{1,3},{3,5},{5,7},{7,1},{8,10},{10,12},{12... | collective-permute-start | bytes 2211848 | tf_op jit(solution)/shard_map/ppermute | solution.py:371
  76.4 50.5 %copy-start.1 = (bf16[64,16384]{1,0:T(8,128)(2,1)S(1)}, bf16[64,16384]{1,0:T(8,128)(2,1)}, u32[]{:S(2)}) copy-start(bf16[64,16384]{1,0:T(8,128)(2,1)} %t_ref.1) | copy-start | bytes 6291460
  89.6 37.3 %all-to-all-start.5 = ((bf16[32,160,128]{2,1,0:T(8,128)(2,1)}), bf16[32,160,128]{2,1,0:T(8,128)(2,1)S(1)}, u32[]{:S(2)}, u32[]{:S(2)}) async-start(bf16[32,160,128]{2,1,0:T(8,128)(2,1)} %bitcast.20), calls=%async_computation.5 | async-start | bytes 2621440 | tf_op jit(solution)/shard_map/all_to_all | solution.py:451
  128.7 1.0 copy-start.2

commit v4 on v3

--- a/solution.py
+++ b/solution.py
@@ -306,9 +306,9 @@
 def contract_kernel(rows, planes, subs, first, last, irrep_s, spin_s, counts, t_ref, *refs):
     v_refs = refs[: last - first]
     if first:
-        out_hbm, v_rows, sums, out_ref, copied = refs[-5:]
+        out_hbm, v_rows, out_ref, copied = refs[-4:]
     else:
-        out_ref, v_rows, sums = refs[-3:]
+        out_ref, v_rows = refs[-2:]
     plane = lax.axis_index("plane")
     mine = lax.axis_index("row") * subs + lax.axis_index("sub")
     n, pairs = out_ref.shape[3:]
@@ -327,15 +327,14 @@
     slot = lax.broadcasted_iota(jnp.int32, (n, rows * pairs), 0)
 
     def one_plane(k, carry):
-        for s in range(3):
-            sums[s] = jnp.dot(v_rows[k], t_ref[s], preferred_element_type=jnp.float32)
         of = lax.rem(plane + shift_of(k + first) + planes, planes)
         for y in range(subs):
             a = of * subs + y
             s = spin_s[a]
             low = counts[jnp.bitwise_xor(irrep_s[a], mine), 0]
-            lower = sums[s, y * n : (y + 1) * n, :]
-            upper = sums[s + 1, y * n : (y + 1) * n, :]
+            block = v_rows[k, y * n : (y + 1) * n, :]
+            lower = jnp.dot(block, t_ref[s], preferred_element_type=jnp.float32)
+            upper = jnp.dot(block, t_ref[s + 1], preferred_element_type=jnp.float32)
             result = jnp.where(slot < low, lower, upper).astype(jnp.bfloat16)
             for r in range(rows):
                 out_ref[r, k if first else of, y] = result[:, r * pairs : (r + 1) * pairs]
@@ -428,7 +427,6 @@
         shape = (rows, planes, subs, cap, group // rows)
         scratch = [
             pltpu.VMEM((last - first, subs * cap, rows * 256 + LANES), jnp.bfloat16),
-            pltpu.VMEM((3, subs * cap, group), jnp.float32),
         ]
         if first:
             scratch += [

time: 130 us -> 130 us (level)
  Pallas kernels: 35.7 us -> 33.9 us
    pallas_call x2, Pallas kernels: 9.89 us -> 8.11 us  [packed(): pl.pallas_call(functools.partial(contract_kernel, rows, planes, subs, fir...]
    ppermute x2, waiting for transfers between devices: 27.4 us -> 28.7 us  [ring_gather(): found[-step] = lax.ppermute(found[1 - step], 'plane', up)]
  transfers between devices with their start and end apart: 6 -> 6, of which waited for: 6 -> 6; matrix products, arithmetic and copies ran while one was open for 0% -> 0% of each run, Pallas kernels for 17% -> 16%
where the time goes in v4:
time: 130 us; the launch traced here: 129 us
  waiting for transfers between devices  73.6 us (57%)
  Pallas kernels  33.9 us (26%)
  starting transfers between devices  16.7 us (13%)
  local copies, waits for them, and re-layouts  2.47 us (2%)
  matrix products  1.74 us (1%)
    all_to_all x1, waiting for transfers between devices, packed(): back = lax.all_to_all(result, all_axes, 0, 0, tiled=True)  32.6 us
    ppermute x2, waiting for transfers between devices, ring_gather(): found[-step] = lax.ppermute(found[1 - step], 'plane', up)  28.7 us
    pallas_call x1, Pallas kernels, local(): pl.pallas_call(functools.partial(pack_integrals_kernel, c_count, c_total,...  10.5 us
    pallas_call x2, Pallas kernels, packed(): pl.pallas_call(functools.partial(contract_kernel, rows, planes, subs, fir...  8.11 us
    pallas_call x1, Pallas kernels, packed(): pl.pallas_call(functools.partial(pack_amplitudes_kernel, c_total, cap), o...  8.07 us
    all_to_all x1, waiting for transfers between devices, packed(): t_mine = lax.all_to_all(t_packed, plane_axes, 0, 0, tiled=True)  7.75 us
    all_to_all x1, starting transfers between devices, packed(): v_plane = lax.all_to_all(v_packed, plane_axes, 0, 0, tiled=True)  5.19 us
    pallas_call x1, Pallas kernels, packed(): pl.pallas_call(functools.partial(unpack_amplitudes_kernel, rows, subs, c_...  5.05 us
  transfers between devices with their start and end apart: 6, of which 6 were waited for; matrix products, arithmetic and copies ran while one was open for 0% of the time, Pallas kernels for 16%

profile of v4, /device:TPU:0, one launch (start us, length us, event | category | flops | bytes accessed | tf_op | source)
XLA Modules:
  0.0 129.2 jit_solution(16582955838466067091)
XLA Ops:
  0.0 0.0 copy-start.3
  0.0 10.5 %pack_integrals.1 = (bf16[8,400,128]{2,1,0:T(8,128)(2,1)}, s32[2,1024]{1,0:T(2,128)S(1)}, s32[20,128]{1,0:T(8,128)S(1)}, s32[16,128]{1,0:T(8,128)S(1)}, s32[1]{0:T(128)}) custom-call(s32[1024]{0:T(1024)} %irrep_s.11, s32[1024]{0:T(1024)} %spin_s.9, s32[1,1024]{1,0:T(1,128)} %bitcast.50, s32[1,1024]{1,0:T(1,128)} %bitcast.51, bf16[1024,4096]{1,0:T(8,128)(2,1)} %v_hbm.1), custom_call_target="tpu_custom_call" | custom-call | flops 8999999488 | tf_op jit(solution)/shard_map/pack_integrals/pallas_call | solution.py:474
  10.5 5.2 %all-to-all-start.4 = ((bf16[8,400,128]{2,1,0:T(8,128)(2,1)}), bf16[8,400,128]{2,1,0:T(8,128)(2,1)S(1)}, u32[]{:S(2)}, u32[]{:S(2)}) async-start(bf16[8,400,128]{2,1,0:T(8,128)(2,1)} %get-tuple-element.41), calls=%async_computation.4 | async-start | bytes 1638400 | tf_op jit(solution)/shard_map/all_to_all | solution.py:385
  15.7 0.0 copy-done.3
  15.7 0.0 copy-start.4
  15.7 8.1 %pack_amplitudes.1 = bf16[8,1280,128]{2,1,0:T(8,128)(2,1)S(1)} custom-call(s32[1024]{0:T(1024)S(1)} %copy-done.3, s32[2,1024]{1,0:T(2,128)S(1)} %get-tuple-element.38.slots, bf16[64,16384]{1,0:T(8,128)(2,1)} %t_ref.1), custom_call_target="tpu_custom_call" | custom-call | flops 8000000000 | tf_op jit(solution)/shard_map/pack_amplitudes/pallas_call | solution.py:396
  23.8 0.0 copy-start
  23.8 1.5 %copy-done = bf16[8,1280,128]{2,1,0:T(8,128)(2,1)} copy-done((bf16[8,1280,128]{2,1,0:T(8,128)(2,1)}, bf16[8,1280,128]{2,1,0:T(8,128)(2,1)S(1)}, u32[]{:S(2)}) %copy-start) | copy-done | bytes 2621464
  25.3 2.5 %all-to-all-done.4.v_ref = bf16[8,400,128]{2,1,0:T(8,128)(2,1)S(1)} async-done(((bf16[8,400,128]{2,1,0:T(8,128)(2,1)}), bf16[8,400,128]{2,1,0:T(8,128)(2,1)S(1)}, u32[]{:S(2)}, u32[]{:S(2)}) %all-to-all-start.4) | async-done | bytes 819232 | tf_op jit(solution)/shard_map/all_to_all | solution.py:385
  27.8 3.6 %all-to-all-start.3 = ((bf16[8,1280,128]{2,1,0:T(8,128)(2,1)}), bf16[8,1280,128]{2,1,0:T(8,128)(2,1)S(1)}, u32[]{:S(2)}, u32[]{:S(2)}) async-start(bf16[8,1280,128]{2,1,0:T(8,128)(2,1)} %copy-done), calls=%async_computation.3 | async-start | bytes 5242880 | tf_op jit(solution)/shard_map/all_to_all | solution.py:409
  31.4 0.0 copy-done.4
  31.4 2.2 %join_tails.1.refs_0_ = bf16[2880,128]{1,0:T(8,128)(2,1)} custom-call(s32[1024]{0:T(1024)S(1)} %copy-done.3, s32[1024]{0:T(1024)S(1)} %copy-done.4, s32[20,128]{1,0:T(8,128)S(1)} %get-tuple-element.40.offsets, s32[16,128]{1,0:T(8,128)S(1)} %get-tuple-element.39.counts, bf16[8,400,128]{2,1,0:T(8,128)(2,1)S(1)} %all-to-all-done.4.v_ref), custom_call_target="tpu_custom_call" | custom-call | flops 1500000000 | tf_op jit(solution)/shard_map/join_tails/pallas_call | solution.py:386
  33.6 1.6 %collective-permute-start = (bf16[2880,128]{1,0:T(8,128)(2,1)}, bf16[2880,128]{1,0:T(8,128)(2,1)S(1)}, u32[]{:S(2)}, u32[]{:S(2)}) collective-permute-start(bf16[2880,128]{1,0:T(8,128)(2,1)} %join_tails.1.refs_0_), channel_id=1, source_target_pairs={{0,2},{2,4},{4,6},{6,0},{1,3},{3,5},{5,7},{7,1},{8,10},{10,12},{12... | collective-permute-start | bytes 2211848 | tf_op jit(solution)/shard_map/ppermute | solution.py:370
  35.2 2.2 %collective-permute-start.2 = (bf16[2880,128]{1,0:T(8,128)(2,1)}, bf16[2880,128]{1,0:T(8,128)(2,1)}, u32[]{:S(2)}, u32[]{:S(2)}) collective-permute-start(bf16[2880,128]{1,0:T(8,128)(2,1)} %join_tails.1.refs_0_), channel_id=1, source_target_pairs={{0,6},{2,0},{4,2},{6,4},{1,7},{3,1},{5,3},{7,5},{8,14},{10,8},{12,... | collective-permute-start | bytes 2211848 | tf_op jit(solution)/shard_map/ppermute | solution.py:372
  37.4 17.5 %collective-permute-done.refs_1_ = bf16[2880,128]{1,0:T(8,128)(2,1)S(1)} collective-permute-done((bf16[2880,128]{1,0:T(8,128)(2,1)}, bf16[2880,128]{1,0:T(8,128)(2,1)S(1)}, u32[]{:S(2)}, u32[]{:S(2)}) %collective-permute-start) | collective-permute-done | bytes 737312 | tf_op jit(solution)/shard_map/ppermute | solution.py:370
  55.0 0.0 collective-permute-start.1
  55.0 7.8 %all-to-all-done.3.t_ref = bf16[8,1280,128]{2,1,0:T(8,128)(2,1)S(1)} async-done(((bf16[8,1280,128]{2,1,0:T(8,128)(2,1)}), bf16[8,1280,128]{2,1,0:T(8,128)(2,1)S(1)}, u32[]{:S(2)}, u32[]{:S(2)}) %all-to-all-start.3) | async-done | bytes 2621472 | tf_op jit(solution)/shard_map/all_to_all | solution.py:409
  62.7 5.0 %unpack_amplitudes.1.t_ref = bf16[3,1152,512]{2,1,0:T(8,128)(2,1)S(1)} custom-call(s32[1024]{0:T(1024)S(1)} %copy-done.3, s32[1024]{0:T(1024)S(1)} %copy-done.4, s32[20,128]{1,0:T(8,128)S(1)} %get-tuple-element.40.offsets, s32[16,128]{1,0:T(8,128)S(1)} %get-tuple-element.39.counts, bf16[8,1280,128]{2,1,0:T(8,128)(2,1)S(1)} %all-to-all-done.3.t_ref), custom_call_target="tpu_custom_call" | custom-call | flops 6000000000 | tf_op jit(solution)/shard_map/unpack_amplitudes/pallas_call | solution.py:410
  67.8 2.1 %collective-permute-done.2.refs_2_ = bf16[2880,128]{1,0:T(8,128)(2,1)} collective-permute-done((bf16[2880,128]{1,0:T(8,128)(2,1)}, bf16[2880,128]{1,0:T(8,128)(2,1)}, u32[]{:S(2)}, u32[]{:S(2)}) %collective-permute-start.2) | collective-permute-done | bytes 737312 | tf_op jit(solution)/shard_map/ppermute | solution.py:372
  69.9 5.2 %contract.2.refs_1_ = bf16[4,4,2,160,128]{4,3,2,1,0:T(8,128)(2,1)} custom-call(s32[1024]{0:T(1024)S(1)} %copy-done.3, s32[1024]{0:T(1024)S(1)} %copy-done.4, s32[16,128]{1,0:T(8,128)S(1)} %get-tuple-element.39.counts, bf16[3,1152,512]{2,1,0:T(8,128)(2,1)S(1)} %unpack_amplitudes.1.t_ref, bf16[2880,128]{1,0:T(8,128)(2,1)} %join_tails.1.refs_0_, ...), custom_call_target="tpu_custom_call" | custom-call | flops 6000000000 | tf_op jit(solution)/shard_map/contract/pallas_call | solution.py:437
  75.1 0.0 copy-start.1
  75.1 11.2 %collective-permute-done.1.refs_0_ = bf16[2880,128]{1,0:T(8,128)(2,1)} collective-permute-done((bf16[2880,128]{1,0:T(8,128)(2,1)S(1)}, bf16[2880,128]{1,0:T(8,128)(2,1)}, u32[]{:S(2)}, u32[]{:S(2)}) %collective-permute-start.1) | collective-permute-done | bytes 737312 | tf_op jit(solution)/shard_map/ppermute | solution.py:370
  86.2 2.9 %contract.3 = bf16[4,4,2,160,128]{4,3,2,1,0:T(8,128)(2,1)} custom-call(s32[1024]{0:T(1024)S(1)} %copy-done.3, s32[1024]{0:T(1024)S(1)} %copy-done.4, s32[16,128]{1,0:T(8,128)S(1)} %get-tuple-element.39.counts, bf16[3,1152,512]{2,1,0:T(8,128)(2,1)S(1)} %unpack_amplitudes.1.t_ref, ...), custom_call_target="tpu_custom_call", output_to_operand_aliasing={{}: (5, {})} | custom-call | flops 2000000000 | tf_op jit(solution)/shard_map/contract/pallas_call | solution.py:437
  89.1 4.1 %all-to-all-start.5 = ((bf16[32,160,128]{2,1,0:T(8,128)(2,1)}), bf16[32,160,128]{2,1,0:T(8,128)(2,1)S(1)}, u32[]{:S(2)}, u32[]{:S(2)}) async-start(bf16[32,160,128]{2,1,0:T(8,128)(2,1)} %bitcast.20), calls=%async_computation.5 | async-start | bytes 2621440 | tf_op jit(solution)/shard_map/all_to_all | solution.py:449
  93.8 32.6 %all-to-all-done.5 = bf16[32,160,128]{2,1,0:T(8,128)(2,1)S(1)} async-done(((bf16[32,160,128]{2,1,0:T(8,128)(2,1)}), bf16[32,160,128]{2,1,0:T(8,128)(2,1)S(1)}, u32[]{:S(2)}, u32[]{:S(2)}) %all-to-all-start.5) | async-done | bytes 1310752 | tf_op jit(solution)/shard_map/all_to_all | solution.py:449
  126.5 0.0 copy-done.1
  126.5 1.8 %conditional.6 = (bf16[512,1024]{1,0:T(8,128)(2,1)S(1)}) conditional(s32[]{:T(128)} %bitcast.19, (s32[1024]{0:T(1024)S(1)}, s32[1024]{0:T(1024)S(1)}, bf16[1024,4096]{1,0:T(8,128)(2,1)}, bf16[64,16384]{1,0:T(8,128)(2,1)S(1)}) %tuple.30, (s32[2,1024]{1,0:T(2,128)S(1)}, bf16[32,160,128]{2,1,0:T(8,128)(2,1)S(1)}) %tuple.22), branch_computations={%region_0.2_spmd, %region_2.3_spmd} | conditional | flops 17189851136 | bytes 171008352
  126.5 1.7 %bitcast_convert_fusion = bf16[1024,4,128]{0,2,1:T(8,128)(2,1)S(1)} fusion(bf16[4,4,2,160,128]{4,3,2,1,0:T(8,128)(2,1)S(1)} %bitcast.47, s32[1024]{0:T(1024)S(1)} %bitcast.53, s32[4,2,160]{2,1,0:T(2,128)S(1)} %multiply_add_fusion.1), kind=kOutput, calls=%fused_computation.16 | convolution fusion | flops 1344012288 | bytes 2368512 | tf_op jit(solution)/shard_map/cond/branch_1_fun/dot_general | solution.py:459
  128.2 0.0 copy-start.2
  128.2 1.0 copy-done.2
  (2 shorter events, 0.0 us)
Async XLA Ops:
  0.0 15.7 %copy-start.3 = (s32[1024]{0:T(1024)S(1)}, s32[1024]{0:T(1024)}, u32[]{:S(2)}) copy-start(s32[1024]{0:T(1024)} %irrep_s.11) | copy-start | bytes 12292
  10.5 17.3 %all-to-all-start.4 = ((bf16[8,400,128]{2,1,0:T(8,128)(2,1)}), bf16[8,400,128]{2,1,0:T(8,128)(2,1)S(1)}, u32[]{:S(2)}, u32[]{:S(2)}) async-start(bf16[8,400,128]{2,1,0:T(8,128)(2,1)} %get-tuple-element.41), calls=%async_computation.4 | async-start | bytes 1638400 | tf_op jit(solution)/shard_map/all_to_all | solution.py:385
  15.7 15.7 %copy-start.4 = (s32[1024]{0:T(1024)S(1)}, s32[1024]{0:T(1024)}, u32[]{:S(2)}) copy-start(s32[1024]{0:T(1024)} %spin_s.9) | copy-start | bytes 12292
  23.8 1.5 %copy-start = (bf16[8,1280,128]{2,1,0:T(8,128)(2,1)}, bf16[8,1280,128]{2,1,0:T(8,128)(2,1)S(1)}, u32[]{:S(2)}) copy-start(bf16[8,1280,128]{2,1,0:T(8,128)(2,1)S(1)} %pack_amplitudes.1) | copy-start | bytes 7864324
  27.8 35.0 %all-to-all-start.3 = ((bf16[8,1280,128]{2,1,0:T(8,128)(2,1)}), bf16[8,1280,128]{2,1,0:T(8,128)(2,1)S(1)}, u32[]{:S(2)}, u32[]{:S(2)}) async-start(bf16[8,1280,128]{2,1,0:T(8,128)(2,1)} %copy-done), calls=%async_computation.3 | async-start | bytes 5242880 | tf_op jit(solution)/shard_map/all_to_all | solution.py:409
  33.6 21.3 %collective-permute-start = (bf16[2880,128]{1,0:T(8,128)(2,1)}, bf16[2880,128]{1,0:T(8,128)(2,1)S(1)}, u32[]{:S(2)}, u32[]{:S(2)}) collective-permute-start(bf16[2880,128]{1,0:T(8,128)(2,1)} %join_tails.1.refs_0_), channel_id=1, source_target_pairs={{0,2},{2,4},{4,6},{6,0},{1,3},{3,5},{5,7},{7,1},{8,10},{10,12},{12... | collective-permute-start | bytes 2211848 | tf_op jit(solution)/shard_map/ppermute | solution.py:370
  35.2 34.7 %collective-permute-start.2 = (bf16[2880,128]{1,0:T(8,128)(2,1)}, bf16[2880,128]{1,0:T(8,128)(2,1)}, u32[]{:S(2)}, u32[]{:S(2)}) collective-permute-start(bf16[2880,128]{1,0:T(8,128)(2,1)} %join_tails.1.refs_0_), channel_id=1, source_target_pairs={{0,6},{2,0},{4,2},{6,4},{1,7},{3,1},{5,3},{7,5},{8,14},{10,8},{12,... | collective-permute-start | bytes 2211848 | tf_op jit(solution)/shard_map/ppermute | solution.py:372
  55.0 31.3 %collective-permute-start.1 = (bf16[2880,128]{1,0:T(8,128)(2,1)S(1)}, bf16[2880,128]{1,0:T(8,128)(2,1)}, u32[]{:S(2)}, u32[]{:S(2)}) collective-permute-start(bf16[2880,128]{1,0:T(8,128)(2,1)S(1)} %collective-permute-done.refs_1_), channel_id=1, source_target_pairs={{0,2},{2,4},{4,6},{6,0},{1,3},{3,5},{5,7},{7,1},{8,10},{10,12},{12... | collective-permute-start | bytes 2211848 | tf_op jit(solution)/shard_map/ppermute | solution.py:370
  75.1 51.4 %copy-start.1 = (bf16[64,16384]{1,0:T(8,128)(2,1)S(1)}, bf16[64,16384]{1,0:T(8,128)(2,1)}, u32[]{:S(2)}) copy-start(bf16[64,16384]{1,0:T(8,128)(2,1)} %t_ref.1) | copy-start | bytes 6291460
  89.1 37.3 %all-to-all-start.5 = ((bf16[32,160,128]{2,1,0:T(8,128)(2,1)}), bf16[32,160,128]{2,1,0:T(8,128)(2,1)S(1)}, u32[]{:S(2)}, u32[]{:S(2)}) async-start(bf16[32,160,128]{2,1,0:T(8,128)(2,1)} %bitcast.20), calls=%async_computation.5 | async-start | bytes 2621440 | tf_op jit(solution)/shard_map/all_to_all | solution.py:449
  128.2 1.0 copy-start.2

commit v5 on v4

--- a/solution.py
+++ b/solution.py
@@ -151,9 +151,9 @@
     tail_ref[...] = jnp.zeros_like(tail_ref)
     lane = lax.broadcasted_iota(jnp.int32, (virtuals, 256), 1)
     tail_lane = 256 + lax.broadcasted_iota(jnp.int32, (virtuals, LANES), 1) % 64
+    longest = [jnp.max(ends_ref[pl.ds(row * c_count + i, 1), :]) for i in range(c_count)]
     main = None
     for i in range(c_count):
-        longest = jnp.max(ends_ref[pl.ds(row * c_count + i, 1), :])
         copies[i].wait()
         masked = jnp.where(
             row_label == cd_label[i : i + 1], v_ref[i], jnp.zeros((), v_ref.dtype)
@@ -164,7 +164,7 @@
         )
         main = term if main is None else main + term
 
-        @pl.when(longest > 256)
+        @pl.when(longest[i] > 256)
         def _(masked=masked, slot=slot):
             tail_ref[...] += jnp.dot(
                 masked,
@@ -279,20 +279,29 @@
     for y in range(subs):
         a = plane * subs + y
         low = counts[jnp.bitwise_xor(irrep_s[a], mine), 0]
-        joined = [jnp.zeros((cap, LANES), jnp.float32) for _ in range(2)]
+        wide = []
         for r in range(rows):
             tail = v_ref[r * subs + y, main:, :]
             none = jnp.zeros((), tail.dtype)
-            wide = jnp.concatenate(
-                [jnp.where(left, tail, none), jnp.where(left, none, tail)], axis=0
+            wide.append(
+                jnp.concatenate(
+                    [jnp.where(left, tail, none), jnp.where(left, none, tail)], axis=0
+                )
             )
-            for k in range(2):
-                over = offsets[c_total + r, mine + 8 * (spin_s[a] + k)]
-                joined[k] += jnp.dot(
-                    wide,
-                    (place + over == lane).astype(jnp.bfloat16),
-                    preferred_element_type=jnp.float32,
+        wide = jnp.concatenate(wide, axis=1)
+        joined = []
+        for k in range(2):
+            places = [
+                (place + offsets[c_total + r, mine + 8 * (spin_s[a] + k)] == lane).astype(
+                    jnp.bfloat16
                 )
+                for r in range(rows)
+            ]
+            joined.append(
+                jnp.dot(
+                    wide, jnp.concatenate(places, axis=0), preferred_element_type=jnp.float32
+                )
+            )
         at = rows * subs * main + y * cap
         out_ref[at : at + cap, :] = jnp.where(slot < low, joined[0], joined[1]).astype(
             jnp.bfloat16

time: 130 us -> 129 us (level)
  no operation moved by 1% of the time
where the time goes in v5:
time: 129 us
  waiting for transfers between devices  73.7 us (57%)
  Pallas kernels  33.4 us (26%)
  starting transfers between devices  16.7 us (13%)
  local copies, waits for them, and re-layouts  2.47 us (2%)
  matrix products  1.74 us (1%)
    all_to_all x1, waiting for transfers between devices, packed(): back = lax.all_to_all(result, all_axes, 0, 0, tiled=True)  32.6 us
    ppermute x2, waiting for transfers between devices, ring_gather(): found[-step] = lax.ppermute(found[1 - step], 'plane', up)  28.7 us
    pallas_call x1, Pallas kernels, local(): pl.pallas_call(functools.partial(pack_integrals_kernel, c_count, c_total,...  10 us
    pallas_call x2, Pallas kernels, packed(): pl.pallas_call(functools.partial(contract_kernel, rows, planes, subs, fir...  8.11 us
    pallas_call x1, Pallas kernels, packed(): pl.pallas_call(functools.partial(pack_amplitudes_kernel, c_total, cap), o...  8.06 us
    all_to_all x1, waiting for transfers between devices, packed(): t_mine = lax.all_to_all(t_packed, plane_axes, 0, 0, tiled=True)  7.75 us
    all_to_all x1, starting transfers between devices, packed(): v_plane = lax.all_to_all(v_packed, plane_axes, 0, 0, tiled=True)  5.19 us
    pallas_call x1, Pallas kernels, packed(): pl.pallas_call(functools.partial(unpack_amplitudes_kernel, rows, subs, c_...  5.05 us
  transfers between devices with their start and end apart: 6, of which 6 were waited for; matrix products, arithmetic and copies ran while one was open for 0% of the time, Pallas kernels for 16%

profile of v5, /device:TPU:0, one launch (start us, length us, event | category | flops | bytes accessed | tf_op | source)
XLA Modules:
  0.0 128.7 jit_solution(15467812401769771516)
XLA Ops:
  0.0 0.0 copy-start.3
  0.0 10.0 %pack_integrals.1 = (bf16[8,400,128]{2,1,0:T(8,128)(2,1)}, s32[2,1024]{1,0:T(2,128)S(1)}, s32[20,128]{1,0:T(8,128)S(1)}, s32[16,128]{1,0:T(8,128)S(1)}, s32[1]{0:T(128)}) custom-call(s32[1024]{0:T(1024)} %irrep_s.11, s32[1024]{0:T(1024)} %spin_s.9, s32[1,1024]{1,0:T(1,128)} %bitcast.50, s32[1,1024]{1,0:T(1,128)} %bitcast.51, bf16[1024,4096]{1,0:T(8,128)(2,1)} %v_hbm.1), custom_call_target="tpu_custom_call" | custom-call | flops 8999999488 | tf_op jit(solution)/shard_map/pack_integrals/pallas_call | solution.py:483
  10.0 5.2 %all-to-all-start.4 = ((bf16[8,400,128]{2,1,0:T(8,128)(2,1)}), bf16[8,400,128]{2,1,0:T(8,128)(2,1)S(1)}, u32[]{:S(2)}, u32[]{:S(2)}) async-start(bf16[8,400,128]{2,1,0:T(8,128)(2,1)} %get-tuple-element.41), calls=%async_computation.4 | async-start | bytes 1638400 | tf_op jit(solution)/shard_map/all_to_all | solution.py:394
  15.2 0.0 copy-done.3
  15.2 0.0 copy-start.4
  15.2 8.1 %pack_amplitudes.1 = bf16[8,1280,128]{2,1,0:T(8,128)(2,1)S(1)} custom-call(s32[1024]{0:T(1024)S(1)} %copy-done.3, s32[2,1024]{1,0:T(2,128)S(1)} %get-tuple-element.38.slots, bf16[64,16384]{1,0:T(8,128)(2,1)} %t_ref.1), custom_call_target="tpu_custom_call" | custom-call | flops 8000000000 | tf_op jit(solution)/shard_map/pack_amplitudes/pallas_call | solution.py:405
  23.3 0.0 copy-start
  23.3 1.5 %copy-done = bf16[8,1280,128]{2,1,0:T(8,128)(2,1)} copy-done((bf16[8,1280,128]{2,1,0:T(8,128)(2,1)}, bf16[8,1280,128]{2,1,0:T(8,128)(2,1)S(1)}, u32[]{:S(2)}) %copy-start) | copy-done | bytes 2621464
  24.8 2.5 %all-to-all-done.4.v_ref = bf16[8,400,128]{2,1,0:T(8,128)(2,1)S(1)} async-done(((bf16[8,400,128]{2,1,0:T(8,128)(2,1)}), bf16[8,400,128]{2,1,0:T(8,128)(2,1)S(1)}, u32[]{:S(2)}, u32[]{:S(2)}) %all-to-all-start.4) | async-done | bytes 819232 | tf_op jit(solution)/shard_map/all_to_all | solution.py:394
  27.3 3.6 %all-to-all-start.3 = ((bf16[8,1280,128]{2,1,0:T(8,128)(2,1)}), bf16[8,1280,128]{2,1,0:T(8,128)(2,1)S(1)}, u32[]{:S(2)}, u32[]{:S(2)}) async-start(bf16[8,1280,128]{2,1,0:T(8,128)(2,1)} %copy-done), calls=%async_computation.3 | async-start | bytes 5242880 | tf_op jit(solution)/shard_map/all_to_all | solution.py:418
  30.9 0.0 copy-done.4
  30.9 2.2 %join_tails.1.refs_0_ = bf16[2880,128]{1,0:T(8,128)(2,1)} custom-call(s32[1024]{0:T(1024)S(1)} %copy-done.3, s32[1024]{0:T(1024)S(1)} %copy-done.4, s32[20,128]{1,0:T(8,128)S(1)} %get-tuple-element.40.offsets, s32[16,128]{1,0:T(8,128)S(1)} %get-tuple-element.39.counts, bf16[8,400,128]{2,1,0:T(8,128)(2,1)S(1)} %all-to-all-done.4.v_ref), custom_call_target="tpu_custom_call" | custom-call | flops 1500000000 | tf_op jit(solution)/shard_map/join_tails/pallas_call | solution.py:395
  33.2 1.6 %collective-permute-start = (bf16[2880,128]{1,0:T(8,128)(2,1)}, bf16[2880,128]{1,0:T(8,128)(2,1)S(1)}, u32[]{:S(2)}, u32[]{:S(2)}) collective-permute-start(bf16[2880,128]{1,0:T(8,128)(2,1)} %join_tails.1.refs_0_), channel_id=1, source_target_pairs={{0,2},{2,4},{4,6},{6,0},{1,3},{3,5},{5,7},{7,1},{8,10},{10,12},{12... | collective-permute-start | bytes 2211848 | tf_op jit(solution)/shard_map/ppermute | solution.py:379
  34.7 2.2 %collective-permute-start.2 = (bf16[2880,128]{1,0:T(8,128)(2,1)}, bf16[2880,128]{1,0:T(8,128)(2,1)}, u32[]{:S(2)}, u32[]{:S(2)}) collective-permute-start(bf16[2880,128]{1,0:T(8,128)(2,1)} %join_tails.1.refs_0_), channel_id=1, source_target_pairs={{0,6},{2,0},{4,2},{6,4},{1,7},{3,1},{5,3},{7,5},{8,14},{10,8},{12,... | collective-permute-start | bytes 2211848 | tf_op jit(solution)/shard_map/ppermute | solution.py:381
  37.0 17.5 %collective-permute-done.refs_1_ = bf16[2880,128]{1,0:T(8,128)(2,1)S(1)} collective-permute-done((bf16[2880,128]{1,0:T(8,128)(2,1)}, bf16[2880,128]{1,0:T(8,128)(2,1)S(1)}, u32[]{:S(2)}, u32[]{:S(2)}) %collective-permute-start) | collective-permute-done | bytes 737312 | tf_op jit(solution)/shard_map/ppermute | solution.py:379
  54.5 0.0 collective-permute-start.1
  54.5 7.8 %all-to-all-done.3.t_ref = bf16[8,1280,128]{2,1,0:T(8,128)(2,1)S(1)} async-done(((bf16[8,1280,128]{2,1,0:T(8,128)(2,1)}), bf16[8,1280,128]{2,1,0:T(8,128)(2,1)S(1)}, u32[]{:S(2)}, u32[]{:S(2)}) %all-to-all-start.3) | async-done | bytes 2621472 | tf_op jit(solution)/shard_map/all_to_all | solution.py:418
  62.3 5.0 %unpack_amplitudes.1.t_ref = bf16[3,1152,512]{2,1,0:T(8,128)(2,1)S(1)} custom-call(s32[1024]{0:T(1024)S(1)} %copy-done.3, s32[1024]{0:T(1024)S(1)} %copy-done.4, s32[20,128]{1,0:T(8,128)S(1)} %get-tuple-element.40.offsets, s32[16,128]{1,0:T(8,128)S(1)} %get-tuple-element.39.counts, bf16[8,1280,128]{2,1,0:T(8,128)(2,1)S(1)} %all-to-all-done.3.t_ref), custom_call_target="tpu_custom_call" | custom-call | flops 6000000000 | tf_op jit(solution)/shard_map/unpack_amplitudes/pallas_call | solution.py:419
  67.3 2.1 %collective-permute-done.2.refs_2_ = bf16[2880,128]{1,0:T(8,128)(2,1)} collective-permute-done((bf16[2880,128]{1,0:T(8,128)(2,1)}, bf16[2880,128]{1,0:T(8,128)(2,1)}, u32[]{:S(2)}, u32[]{:S(2)}) %collective-permute-start.2) | collective-permute-done | bytes 737312 | tf_op jit(solution)/shard_map/ppermute | solution.py:381
  69.4 5.2 %contract.2.refs_1_ = bf16[4,4,2,160,128]{4,3,2,1,0:T(8,128)(2,1)} custom-call(s32[1024]{0:T(1024)S(1)} %copy-done.3, s32[1024]{0:T(1024)S(1)} %copy-done.4, s32[16,128]{1,0:T(8,128)S(1)} %get-tuple-element.39.counts, bf16[3,1152,512]{2,1,0:T(8,128)(2,1)S(1)} %unpack_amplitudes.1.t_ref, bf16[2880,128]{1,0:T(8,128)(2,1)} %join_tails.1.refs_0_, ...), custom_call_target="tpu_custom_call" | custom-call | flops 6000000000 | tf_op jit(solution)/shard_map/contract/pallas_call | solution.py:446
  74.6 0.0 copy-start.1
  74.6 11.2 %collective-permute-done.1.refs_0_ = bf16[2880,128]{1,0:T(8,128)(2,1)} collective-permute-done((bf16[2880,128]{1,0:T(8,128)(2,1)S(1)}, bf16[2880,128]{1,0:T(8,128)(2,1)}, u32[]{:S(2)}, u32[]{:S(2)}) %collective-permute-start.1) | collective-permute-done | bytes 737312 | tf_op jit(solution)/shard_map/ppermute | solution.py:379
  85.8 2.9 %contract.3 = bf16[4,4,2,160,128]{4,3,2,1,0:T(8,128)(2,1)} custom-call(s32[1024]{0:T(1024)S(1)} %copy-done.3, s32[1024]{0:T(1024)S(1)} %copy-done.4, s32[16,128]{1,0:T(8,128)S(1)} %get-tuple-element.39.counts, bf16[3,1152,512]{2,1,0:T(8,128)(2,1)S(1)} %unpack_amplitudes.1.t_ref, ...), custom_call_target="tpu_custom_call", output_to_operand_aliasing={{}: (5, {})} | custom-call | flops 2000000000 | tf_op jit(solution)/shard_map/contract/pallas_call | solution.py:446
  88.7 4.1 %all-to-all-start.5 = ((bf16[32,160,128]{2,1,0:T(8,128)(2,1)}), bf16[32,160,128]{2,1,0:T(8,128)(2,1)S(1)}, u32[]{:S(2)}, u32[]{:S(2)}) async-start(bf16[32,160,128]{2,1,0:T(8,128)(2,1)} %bitcast.20), calls=%async_computation.5 | async-start | bytes 2621440 | tf_op jit(solution)/shard_map/all_to_all | solution.py:458
  93.4 32.6 %all-to-all-done.5 = bf16[32,160,128]{2,1,0:T(8,128)(2,1)S(1)} async-done(((bf16[32,160,128]{2,1,0:T(8,128)(2,1)}), bf16[32,160,128]{2,1,0:T(8,128)(2,1)S(1)}, u32[]{:S(2)}, u32[]{:S(2)}) %all-to-all-start.5) | async-done | bytes 1310752 | tf_op jit(solution)/shard_map/all_to_all | solution.py:458
  126.0 0.0 copy-done.1
  126.0 1.8 %conditional.6 = (bf16[512,1024]{1,0:T(8,128)(2,1)S(1)}) conditional(s32[]{:T(128)} %bitcast.19, (s32[1024]{0:T(1024)S(1)}, s32[1024]{0:T(1024)S(1)}, bf16[1024,4096]{1,0:T(8,128)(2,1)}, bf16[64,16384]{1,0:T(8,128)(2,1)S(1)}) %tuple.30, (s32[2,1024]{1,0:T(2,128)S(1)}, bf16[32,160,128]{2,1,0:T(8,128)(2,1)S(1)}) %tuple.22), branch_computations={%region_0.2_spmd, %region_2.3_spmd} | conditional | flops 17189851136 | bytes 171008352
  126.0 1.7 %bitcast_convert_fusion = bf16[1024,4,128]{0,2,1:T(8,128)(2,1)S(1)} fusion(bf16[4,4,2,160,128]{4,3,2,1,0:T(8,128)(2,1)S(1)} %bitcast.47, s32[1024]{0:T(1024)S(1)} %bitcast.53, s32[4,2,160]{2,1,0:T(2,128)S(1)} %multiply_add_fusion.1), kind=kOutput, calls=%fused_computation.16 | convolution fusion | flops 1344012288 | bytes 2368512 | tf_op jit(solution)/shard_map/cond/branch_1_fun/dot_general | solution.py:468
  127.8 0.0 copy-start.2
  127.8 1.0 copy-done.2
  (2 shorter events, 0.0 us)
Async XLA Ops:
  0.0 15.2 %copy-start.3 = (s32[1024]{0:T(1024)S(1)}, s32[1024]{0:T(1024)}, u32[]{:S(2)}) copy-start(s32[1024]{0:T(1024)} %irrep_s.11) | copy-start | bytes 12292
  10.0 17.3 %all-to-all-start.4 = ((bf16[8,400,128]{2,1,0:T(8,128)(2,1)}), bf16[8,400,128]{2,1,0:T(8,128)(2,1)S(1)}, u32[]{:S(2)}, u32[]{:S(2)}) async-start(bf16[8,400,128]{2,1,0:T(8,128)(2,1)} %get-tuple-element.41), calls=%async_computation.4 | async-start | bytes 1638400 | tf_op jit(solution)/shard_map/all_to_all | solution.py:394
  15.2 15.7 %copy-start.4 = (s32[1024]{0:T(1024)S(1)}, s32[1024]{0:T(1024)}, u32[]{:S(2)}) copy-start(s32[1024]{0:T(1024)} %spin_s.9) | copy-start | bytes 12292
  23.3 1.5 %copy-start = (bf16[8,1280,128]{2,1,0:T(8,128)(2,1)}, bf16[8,1280,128]{2,1,0:T(8,128)(2,1)S(1)}, u32[]{:S(2)}) copy-start(bf16[8,1280,128]{2,1,0:T(8,128)(2,1)S(1)} %pack_amplitudes.1) | copy-start | bytes 7864324
  27.3 35.0 %all-to-all-start.3 = ((bf16[8,1280,128]{2,1,0:T(8,128)(2,1)}), bf16[8,1280,128]{2,1,0:T(8,128)(2,1)S(1)}, u32[]{:S(2)}, u32[]{:S(2)}) async-start(bf16[8,1280,128]{2,1,0:T(8,128)(2,1)} %copy-done), calls=%async_computation.3 | async-start | bytes 5242880 | tf_op jit(solution)/shard_map/all_to_all | solution.py:418
  33.2 21.3 %collective-permute-start = (bf16[2880,128]{1,0:T(8,128)(2,1)}, bf16[2880,128]{1,0:T(8,128)(2,1)S(1)}, u32[]{:S(2)}, u32[]{:S(2)}) collective-permute-start(bf16[2880,128]{1,0:T(8,128)(2,1)} %join_tails.1.refs_0_), channel_id=1, source_target_pairs={{0,2},{2,4},{4,6},{6,0},{1,3},{3,5},{5,7},{7,1},{8,10},{10,12},{12... | collective-permute-start | bytes 2211848 | tf_op jit(solution)/shard_map/ppermute | solution.py:379
  34.7 34.7 %collective-permute-start.2 = (bf16[2880,128]{1,0:T(8,128)(2,1)}, bf16[2880,128]{1,0:T(8,128)(2,1)}, u32[]{:S(2)}, u32[]{:S(2)}) collective-permute-start(bf16[2880,128]{1,0:T(8,128)(2,1)} %join_tails.1.refs_0_), channel_id=1, source_target_pairs={{0,6},{2,0},{4,2},{6,4},{1,7},{3,1},{5,3},{7,5},{8,14},{10,8},{12,... | collective-permute-start | bytes 2211848 | tf_op jit(solution)/shard_map/ppermute | solution.py:381
  54.5 31.3 %collective-permute-start.1 = (bf16[2880,128]{1,0:T(8,128)(2,1)S(1)}, bf16[2880,128]{1,0:T(8,128)(2,1)}, u32[]{:S(2)}, u32[]{:S(2)}) collective-permute-start(bf16[2880,128]{1,0:T(8,128)(2,1)S(1)} %collective-permute-done.refs_1_), channel_id=1, source_target_pairs={{0,2},{2,4},{4,6},{6,0},{1,3},{3,5},{5,7},{7,1},{8,10},{10,12},{12... | collective-permute-start | bytes 2211848 | tf_op jit(solution)/shard_map/ppermute | solution.py:379
  74.6 51.4 %copy-start.1 = (bf16[64,16384]{1,0:T(8,128)(2,1)S(1)}, bf16[64,16384]{1,0:T(8,128)(2,1)}, u32[]{:S(2)}) copy-start(bf16[64,16384]{1,0:T(8,128)(2,1)} %t_ref.1) | copy-start | bytes 6291460
  88.7 37.3 %all-to-all-start.5 = ((bf16[32,160,128]{2,1,0:T(8,128)(2,1)}), bf16[32,160,128]{2,1,0:T(8,128)(2,1)S(1)}, u32[]{:S(2)}, u32[]{:S(2)}) async-start(bf16[32,160,128]{2,1,0:T(8,128)(2,1)} %bitcast.20), calls=%async_computation.5 | async-start | bytes 2621440 | tf_op jit(solution)/shard_map/all_to_all | solution.py:458
  127.8 1.0 copy-start.2

commit v6 on v5

--- a/solution.py
+++ b/solution.py
@@ -121,10 +121,6 @@
         offsets_out[c_total + r : c_total + r + 1, :] = over
         last = (r + 1) * c_count - 1
         over = over + jnp.maximum(ends[last : last + 1, :] - 256, 0)
-    irrep_most = jnp.max(counts[:IRREPS] + counts[IRREPS:])
-    fit = (irrep_most <= cap) & (jnp.max(ends) <= label_cap) & (jnp.max(over) <= LANES)
-    fits_out[0] = jnp.where(fit, 1, 0)
-
     row_label = jnp.bitwise_xor(irrep, irrep_s[a]) + 8 * (spin + spin_s[a])
     row_slot = jnp.bitwise_xor(irrep, irrep_s[a]) * cap + rank8
     slots_out[0:1, :] = row_slot
@@ -152,6 +148,9 @@
     lane = lax.broadcasted_iota(jnp.int32, (virtuals, 256), 1)
     tail_lane = 256 + lax.broadcasted_iota(jnp.int32, (virtuals, LANES), 1) % 64
     longest = [jnp.max(ends_ref[pl.ds(row * c_count + i, 1), :]) for i in range(c_count)]
+    irrep_most = jnp.max(counts[:IRREPS] + counts[IRREPS:])
+    fit = (irrep_most <= cap) & (jnp.max(ends) <= label_cap) & (jnp.max(over) <= LANES)
+    fits_out[0] = jnp.where(fit, 1, 0)
     main = None
     for i in range(c_count):
         copies[i].wait()

time: 129 us -> 129 us (level)
  no operation moved by 1% of the time
where the time goes in v6:
time: 129 us
  waiting for transfers between devices  73.7 us (57%)
  Pallas kernels  33.4 us (26%)
  starting transfers between devices  16.7 us (13%)
  local copies, waits for them, and re-layouts  2.47 us (2%)
  matrix products  1.74 us (1%)
    all_to_all x1, waiting for transfers between devices, packed(): back = lax.all_to_all(result, all_axes, 0, 0, tiled=True)  32.6 us
    ppermute x2, waiting for transfers between devices, ring_gather(): found[-step] = lax.ppermute(found[1 - step], 'plane', up)  28.7 us
    pallas_call x1, Pallas kernels, local(): pl.pallas_call(functools.partial(pack_integrals_kernel, c_count, c_total,...  10 us
    pallas_call x2, Pallas kernels, packed(): pl.pallas_call(functools.partial(contract_kernel, rows, planes, subs, fir...  8.11 us
    pallas_call x1, Pallas kernels, packed(): pl.pallas_call(functools.partial(pack_amplitudes_kernel, c_total, cap), o...  8.07 us
    all_to_all x1, waiting for transfers between devices, packed(): t_mine = lax.all_to_all(t_packed, plane_axes, 0, 0, tiled=True)  7.75 us
    all_to_all x1, starting transfers between devices, packed(): v_plane = lax.all_to_all(v_packed, plane_axes, 0, 0, tiled=True)  5.19 us
    pallas_call x1, Pallas kernels, packed(): pl.pallas_call(functools.partial(unpack_amplitudes_kernel, rows, subs, c_...  5.05 us
  transfers between devices with their start and end apart: 6, of which 6 were waited for; matrix products, arithmetic and copies ran while one was open for 0% of the time, Pallas kernels for 16%

profile of v6, /device:TPU:0, one launch (start us, length us, event | category | flops | bytes accessed | tf_op | source)
XLA Modules:
  0.0 128.7 jit_solution(12806767253233783087)
XLA Ops:
  0.0 0.0 copy-start.3
  0.0 10.0 %pack_integrals.1 = (bf16[8,400,128]{2,1,0:T(8,128)(2,1)}, s32[2,1024]{1,0:T(2,128)S(1)}, s32[20,128]{1,0:T(8,128)S(1)}, s32[16,128]{1,0:T(8,128)S(1)}, s32[1]{0:T(128)}) custom-call(s32[1024]{0:T(1024)} %irrep_s.11, s32[1024]{0:T(1024)} %spin_s.9, s32[1,1024]{1,0:T(1,128)} %bitcast.50, s32[1,1024]{1,0:T(1,128)} %bitcast.51, bf16[1024,4096]{1,0:T(8,128)(2,1)} %v_hbm.1), custom_call_target="tpu_custom_call" | custom-call | flops 8999999488 | tf_op jit(solution)/shard_map/pack_integrals/pallas_call | solution.py:482
  10.0 5.2 %all-to-all-start.4 = ((bf16[8,400,128]{2,1,0:T(8,128)(2,1)}), bf16[8,400,128]{2,1,0:T(8,128)(2,1)S(1)}, u32[]{:S(2)}, u32[]{:S(2)}) async-start(bf16[8,400,128]{2,1,0:T(8,128)(2,1)} %get-tuple-element.41), calls=%async_computation.4 | async-start | bytes 1638400 | tf_op jit(solution)/shard_map/all_to_all | solution.py:393
  15.2 0.0 copy-done.3
  15.2 0.0 copy-start.4
  15.2 8.1 %pack_amplitudes.1 = bf16[8,1280,128]{2,1,0:T(8,128)(2,1)S(1)} custom-call(s32[1024]{0:T(1024)S(1)} %copy-done.3, s32[2,1024]{1,0:T(2,128)S(1)} %get-tuple-element.38.slots, bf16[64,16384]{1,0:T(8,128)(2,1)} %t_ref.1), custom_call_target="tpu_custom_call" | custom-call | flops 8000000000 | tf_op jit(solution)/shard_map/pack_amplitudes/pallas_call | solution.py:404
  23.3 0.0 copy-start
  23.3 1.5 %copy-done = bf16[8,1280,128]{2,1,0:T(8,128)(2,1)} copy-done((bf16[8,1280,128]{2,1,0:T(8,128)(2,1)}, bf16[8,1280,128]{2,1,0:T(8,128)(2,1)S(1)}, u32[]{:S(2)}) %copy-start) | copy-done | bytes 2621464
  24.8 2.5 %all-to-all-done.4.v_ref = bf16[8,400,128]{2,1,0:T(8,128)(2,1)S(1)} async-done(((bf16[8,400,128]{2,1,0:T(8,128)(2,1)}), bf16[8,400,128]{2,1,0:T(8,128)(2,1)S(1)}, u32[]{:S(2)}, u32[]{:S(2)}) %all-to-all-start.4) | async-done | bytes 819232 | tf_op jit(solution)/shard_map/all_to_all | solution.py:393
  27.3 3.6 %all-to-all-start.3 = ((bf16[8,1280,128]{2,1,0:T(8,128)(2,1)}), bf16[8,1280,128]{2,1,0:T(8,128)(2,1)S(1)}, u32[]{:S(2)}, u32[]{:S(2)}) async-start(bf16[8,1280,128]{2,1,0:T(8,128)(2,1)} %copy-done), calls=%async_computation.3 | async-start | bytes 5242880 | tf_op jit(solution)/shard_map/all_to_all | solution.py:417
  30.9 0.0 copy-done.4
  30.9 2.2 %join_tails.1.refs_0_ = bf16[2880,128]{1,0:T(8,128)(2,1)} custom-call(s32[1024]{0:T(1024)S(1)} %copy-done.3, s32[1024]{0:T(1024)S(1)} %copy-done.4, s32[20,128]{1,0:T(8,128)S(1)} %get-tuple-element.40.offsets, s32[16,128]{1,0:T(8,128)S(1)} %get-tuple-element.39.counts, bf16[8,400,128]{2,1,0:T(8,128)(2,1)S(1)} %all-to-all-done.4.v_ref), custom_call_target="tpu_custom_call" | custom-call | flops 1500000000 | tf_op jit(solution)/shard_map/join_tails/pallas_call | solution.py:394
  33.2 1.6 %collective-permute-start = (bf16[2880,128]{1,0:T(8,128)(2,1)}, bf16[2880,128]{1,0:T(8,128)(2,1)S(1)}, u32[]{:S(2)}, u32[]{:S(2)}) collective-permute-start(bf16[2880,128]{1,0:T(8,128)(2,1)} %join_tails.1.refs_0_), channel_id=1, source_target_pairs={{0,2},{2,4},{4,6},{6,0},{1,3},{3,5},{5,7},{7,1},{8,10},{10,12},{12... | collective-permute-start | bytes 2211848 | tf_op jit(solution)/shard_map/ppermute | solution.py:378
  34.7 2.2 %collective-permute-start.2 = (bf16[2880,128]{1,0:T(8,128)(2,1)}, bf16[2880,128]{1,0:T(8,128)(2,1)}, u32[]{:S(2)}, u32[]{:S(2)}) collective-permute-start(bf16[2880,128]{1,0:T(8,128)(2,1)} %join_tails.1.refs_0_), channel_id=1, source_target_pairs={{0,6},{2,0},{4,2},{6,4},{1,7},{3,1},{5,3},{7,5},{8,14},{10,8},{12,... | collective-permute-start | bytes 2211848 | tf_op jit(solution)/shard_map/ppermute | solution.py:380
  37.0 17.5 %collective-permute-done.refs_1_ = bf16[2880,128]{1,0:T(8,128)(2,1)S(1)} collective-permute-done((bf16[2880,128]{1,0:T(8,128)(2,1)}, bf16[2880,128]{1,0:T(8,128)(2,1)S(1)}, u32[]{:S(2)}, u32[]{:S(2)}) %collective-permute-start) | collective-permute-done | bytes 737312 | tf_op jit(solution)/shard_map/ppermute | solution.py:378
  54.5 0.0 collective-permute-start.1
  54.5 7.7 %all-to-all-done.3.t_ref = bf16[8,1280,128]{2,1,0:T(8,128)(2,1)S(1)} async-done(((bf16[8,1280,128]{2,1,0:T(8,128)(2,1)}), bf16[8,1280,128]{2,1,0:T(8,128)(2,1)S(1)}, u32[]{:S(2)}, u32[]{:S(2)}) %all-to-all-start.3) | async-done | bytes 2621472 | tf_op jit(solution)/shard_map/all_to_all | solution.py:417
  62.3 5.0 %unpack_amplitudes.1.t_ref = bf16[3,1152,512]{2,1,0:T(8,128)(2,1)S(1)} custom-call(s32[1024]{0:T(1024)S(1)} %copy-done.3, s32[1024]{0:T(1024)S(1)} %copy-done.4, s32[20,128]{1,0:T(8,128)S(1)} %get-tuple-element.40.offsets, s32[16,128]{1,0:T(8,128)S(1)} %get-tuple-element.39.counts, bf16[8,1280,128]{2,1,0:T(8,128)(2,1)S(1)} %all-to-all-done.3.t_ref), custom_call_target="tpu_custom_call" | custom-call | flops 6000000000 | tf_op jit(solution)/shard_map/unpack_amplitudes/pallas_call | solution.py:418
  67.3 2.1 %collective-permute-done.2.refs_2_ = bf16[2880,128]{1,0:T(8,128)(2,1)} collective-permute-done((bf16[2880,128]{1,0:T(8,128)(2,1)}, bf16[2880,128]{1,0:T(8,128)(2,1)}, u32[]{:S(2)}, u32[]{:S(2)}) %collective-permute-start.2) | collective-permute-done | bytes 737312 | tf_op jit(solution)/shard_map/ppermute | solution.py:380
  69.4 5.2 %contract.2.refs_1_ = bf16[4,4,2,160,128]{4,3,2,1,0:T(8,128)(2,1)} custom-call(s32[1024]{0:T(1024)S(1)} %copy-done.3, s32[1024]{0:T(1024)S(1)} %copy-done.4, s32[16,128]{1,0:T(8,128)S(1)} %get-tuple-element.39.counts, bf16[3,1152,512]{2,1,0:T(8,128)(2,1)S(1)} %unpack_amplitudes.1.t_ref, bf16[2880,128]{1,0:T(8,128)(2,1)} %join_tails.1.refs_0_, ...), custom_call_target="tpu_custom_call" | custom-call | flops 6000000000 | tf_op jit(solution)/shard_map/contract/pallas_call | solution.py:445
  74.6 0.0 copy-start.1
  74.6 11.2 %collective-permute-done.1.refs_0_ = bf16[2880,128]{1,0:T(8,128)(2,1)} collective-permute-done((bf16[2880,128]{1,0:T(8,128)(2,1)S(1)}, bf16[2880,128]{1,0:T(8,128)(2,1)}, u32[]{:S(2)}, u32[]{:S(2)}) %collective-permute-start.1) | collective-permute-done | bytes 737312 | tf_op jit(solution)/shard_map/ppermute | solution.py:378
  85.8 2.9 %contract.3 = bf16[4,4,2,160,128]{4,3,2,1,0:T(8,128)(2,1)} custom-call(s32[1024]{0:T(1024)S(1)} %copy-done.3, s32[1024]{0:T(1024)S(1)} %copy-done.4, s32[16,128]{1,0:T(8,128)S(1)} %get-tuple-element.39.counts, bf16[3,1152,512]{2,1,0:T(8,128)(2,1)S(1)} %unpack_amplitudes.1.t_ref, ...), custom_call_target="tpu_custom_call", output_to_operand_aliasing={{}: (5, {})} | custom-call | flops 2000000000 | tf_op jit(solution)/shard_map/contract/pallas_call | solution.py:445
  88.7 4.1 %all-to-all-start.5 = ((bf16[32,160,128]{2,1,0:T(8,128)(2,1)}), bf16[32,160,128]{2,1,0:T(8,128)(2,1)S(1)}, u32[]{:S(2)}, u32[]{:S(2)}) async-start(bf16[32,160,128]{2,1,0:T(8,128)(2,1)} %bitcast.20), calls=%async_computation.5 | async-start | bytes 2621440 | tf_op jit(solution)/shard_map/all_to_all | solution.py:457
  93.4 32.6 %all-to-all-done.5 = bf16[32,160,128]{2,1,0:T(8,128)(2,1)S(1)} async-done(((bf16[32,160,128]{2,1,0:T(8,128)(2,1)}), bf16[32,160,128]{2,1,0:T(8,128)(2,1)S(1)}, u32[]{:S(2)}, u32[]{:S(2)}) %all-to-all-start.5) | async-done | bytes 1310752 | tf_op jit(solution)/shard_map/all_to_all | solution.py:457
  126.0 0.0 copy-done.1
  126.0 1.8 %conditional.6 = (bf16[512,1024]{1,0:T(8,128)(2,1)S(1)}) conditional(s32[]{:T(128)} %bitcast.19, (s32[1024]{0:T(1024)S(1)}, s32[1024]{0:T(1024)S(1)}, bf16[1024,4096]{1,0:T(8,128)(2,1)}, bf16[64,16384]{1,0:T(8,128)(2,1)S(1)}) %tuple.30, (s32[2,1024]{1,0:T(2,128)S(1)}, bf16[32,160,128]{2,1,0:T(8,128)(2,1)S(1)}) %tuple.22), branch_computations={%region_0.2_spmd, %region_2.3_spmd} | conditional | flops 17189851136 | bytes 171008352
  126.0 1.7 %bitcast_convert_fusion = bf16[1024,4,128]{0,2,1:T(8,128)(2,1)S(1)} fusion(bf16[4,4,2,160,128]{4,3,2,1,0:T(8,128)(2,1)S(1)} %bitcast.47, s32[1024]{0:T(1024)S(1)} %bitcast.53, s32[4,2,160]{2,1,0:T(2,128)S(1)} %multiply_add_fusion.1), kind=kOutput, calls=%fused_computation.16 | convolution fusion | flops 1344012288 | bytes 2368512 | tf_op jit(solution)/shard_map/cond/branch_1_fun/dot_general | solution.py:467
  127.8 0.0 copy-start.2
  127.8 1.0 copy-done.2
  (2 shorter events, 0.0 us)
Async XLA Ops:
  0.0 15.2 %copy-start.3 = (s32[1024]{0:T(1024)S(1)}, s32[1024]{0:T(1024)}, u32[]{:S(2)}) copy-start(s32[1024]{0:T(1024)} %irrep_s.11) | copy-start | bytes 12292
  10.0 17.3 %all-to-all-start.4 = ((bf16[8,400,128]{2,1,0:T(8,128)(2,1)}), bf16[8,400,128]{2,1,0:T(8,128)(2,1)S(1)}, u32[]{:S(2)}, u32[]{:S(2)}) async-start(bf16[8,400,128]{2,1,0:T(8,128)(2,1)} %get-tuple-element.41), calls=%async_computation.4 | async-start | bytes 1638400 | tf_op jit(solution)/shard_map/all_to_all | solution.py:393
  15.2 15.7 %copy-start.4 = (s32[1024]{0:T(1024)S(1)}, s32[1024]{0:T(1024)}, u32[]{:S(2)}) copy-start(s32[1024]{0:T(1024)} %spin_s.9) | copy-start | bytes 12292
  23.3 1.5 %copy-start = (bf16[8,1280,128]{2,1,0:T(8,128)(2,1)}, bf16[8,1280,128]{2,1,0:T(8,128)(2,1)S(1)}, u32[]{:S(2)}) copy-start(bf16[8,1280,128]{2,1,0:T(8,128)(2,1)S(1)} %pack_amplitudes.1) | copy-start | bytes 7864324
  27.3 35.0 %all-to-all-start.3 = ((bf16[8,1280,128]{2,1,0:T(8,128)(2,1)}), bf16[8,1280,128]{2,1,0:T(8,128)(2,1)S(1)}, u32[]{:S(2)}, u32[]{:S(2)}) async-start(bf16[8,1280,128]{2,1,0:T(8,128)(2,1)} %copy-done), calls=%async_computation.3 | async-start | bytes 5242880 | tf_op jit(solution)/shard_map/all_to_all | solution.py:417
  33.2 21.3 %collective-permute-start = (bf16[2880,128]{1,0:T(8,128)(2,1)}, bf16[2880,128]{1,0:T(8,128)(2,1)S(1)}, u32[]{:S(2)}, u32[]{:S(2)}) collective-permute-start(bf16[2880,128]{1,0:T(8,128)(2,1)} %join_tails.1.refs_0_), channel_id=1, source_target_pairs={{0,2},{2,4},{4,6},{6,0},{1,3},{3,5},{5,7},{7,1},{8,10},{10,12},{12... | collective-permute-start | bytes 2211848 | tf_op jit(solution)/shard_map/ppermute | solution.py:378
  34.7 34.7 %collective-permute-start.2 = (bf16[2880,128]{1,0:T(8,128)(2,1)}, bf16[2880,128]{1,0:T(8,128)(2,1)}, u32[]{:S(2)}, u32[]{:S(2)}) collective-permute-start(bf16[2880,128]{1,0:T(8,128)(2,1)} %join_tails.1.refs_0_), channel_id=1, source_target_pairs={{0,6},{2,0},{4,2},{6,4},{1,7},{3,1},{5,3},{7,5},{8,14},{10,8},{12,... | collective-permute-start | bytes 2211848 | tf_op jit(solution)/shard_map/ppermute | solution.py:380
  54.5 31.3 %collective-permute-start.1 = (bf16[2880,128]{1,0:T(8,128)(2,1)S(1)}, bf16[2880,128]{1,0:T(8,128)(2,1)}, u32[]{:S(2)}, u32[]{:S(2)}) collective-permute-start(bf16[2880,128]{1,0:T(8,128)(2,1)S(1)} %collective-permute-done.refs_1_), channel_id=1, source_target_pairs={{0,2},{2,4},{4,6},{6,0},{1,3},{3,5},{5,7},{7,1},{8,10},{10,12},{12... | collective-permute-start | bytes 2211848 | tf_op jit(solution)/shard_map/ppermute | solution.py:378
  74.6 51.4 %copy-start.1 = (bf16[64,16384]{1,0:T(8,128)(2,1)S(1)}, bf16[64,16384]{1,0:T(8,128)(2,1)}, u32[]{:S(2)}) copy-start(bf16[64,16384]{1,0:T(8,128)(2,1)} %t_ref.1) | copy-start | bytes 6291460
  88.7 37.3 %all-to-all-start.5 = ((bf16[32,160,128]{2,1,0:T(8,128)(2,1)}), bf16[32,160,128]{2,1,0:T(8,128)(2,1)S(1)}, u32[]{:S(2)}, u32[]{:S(2)}) async-start(bf16[32,160,128]{2,1,0:T(8,128)(2,1)} %bitcast.20), calls=%async_computation.5 | async-start | bytes 2621440 | tf_op jit(solution)/shard_map/all_to_all | solution.py:457
  127.8 1.0 copy-start.2
